TPU v7x, 32 devices: a whole 2x2x4 slice. The times are simulated.
32 devices in a mesh: seq: 8 (over z, x), ch: 4 (over y, core).
Axes of the slice: x: 2, y: 2, z: 4, core: 2. Of those that a mesh axis runs over, the one named last changes fastest.
Arguments:
- query_rows: float32 [4096, 2048], P('seq', 'ch'), may hold values from -6 to 6
- key_rows: float32 [4096, 2048], P('seq', 'ch'), may hold values from -6 to 6
- value_rows: float32 [4096, 2048], P('seq', 'ch'), may hold values from -6 to 6
- filters: float32 [4096, 2048], P('seq', 'ch'), may hold values from -0.09375 to 0.09375
- skip_gain: float32 [2048], P('ch'), may hold values from -4 to 4
- out_weight: float32 [2048, 2048], P('ch'), may hold values from -0.125 to 0.125
Outputs:
- projected: float32 [2048, 4096], P('ch', 'seq')
All inputs are finite; a program needn't handle non-finite values.
Results may differ from a plain program's by a relative error of at most 0.00007.
Values sent between devices are 32-bit elements; how exact they have to be, the bound alone decides.
No kernel may reach another device: no remote copies, remote signals or barrier semaphores. Data moves between devices by JAX's collectives and lax.ppermute only.
A program may use at most 64 MiB of HBM per device.

v0:
```python
import functools
import math

import jax
import jax.numpy as jnp
import ml_dtypes
import numpy as np
from jax import lax
from jax.experimental import pallas as pl
from jax.experimental.pallas import tpu as pltpu
from jax.sharding import PartitionSpec as P

LANES = 128
MIB = 1024 * 1024
CHUNKS = 1

f32 = jnp.float32
bf16 = jnp.bfloat16


def halves(x):
    high = x.astype(bf16)
    return high, (x - high.astype(f32)).astype(bf16)


def dot(a, b):
    return jnp.dot(a, b, preferred_element_type=f32)


def dot_split(a_high, a_low, b_high, b_low):
    return dot(a_high, b_high) + (dot(a_low, b_high) + dot(a_high, b_low))


def split_table(table):
    high = table.astype(np.float32).astype(ml_dtypes.bfloat16)
    low = (table - high.astype(np.float64)).astype(np.float32).astype(ml_dtypes.bfloat16)
    return jnp.asarray(high), jnp.asarray(low)


def transforms(length):
    orders = np.concatenate([np.arange(0, length, 2), np.arange(1, length, 2)])
    angle = math.pi / length * (orders[None, :] + 0.5) * np.arange(length)[:, None]
    forward = np.concatenate([np.cos(angle), -np.sin(angle)], axis=1)
    return split_table(forward), split_table(forward.T / length)


def call(body, out_shape, *, grid_spec=None, in_specs=None, out_specs=None, scratch=(), room=16, aliases=None, work=1):
    params = pltpu.CompilerParams(vmem_limit_bytes=room * MIB)
    cost = pl.CostEstimate(flops=work, bytes_accessed=1, transcendentals=0)
    kwargs = dict(out_shape=out_shape, compiler_params=params, cost_estimate=cost)
    if aliases:
        kwargs["input_output_aliases"] = aliases
    if grid_spec is not None:
        return pl.pallas_call(body, grid_spec=grid_spec, **kwargs)
    return pl.pallas_call(body, in_specs=in_specs, out_specs=out_specs, scratch_shapes=list(scratch), **kwargs)


def pack_body(group, slim, chunks, me_ref, key_ref, value_ref, filter_ref, *rest):
    outs, (gated, taps) = rest[:-2], rest[-2:]
    part = slim // chunks
    gated[...] = (key_ref[...] * value_ref[...]).T
    taps[...] = filter_ref[...].T
    low = lax.rem(me_ref[0], group)
    for e in range(group):
        start = jnp.bitwise_xor(low, e) * slim
        for k in range(chunks):
            rows = pl.ds(pl.multiple_of(start + k * part, 8), part)
            out = outs[e * chunks + k]
            out[0:part, :] = gated[rows, :]
            out[part : 2 * part, :] = taps[rows, :]


def pack(me, key_rows, value_rows, filters, t, group, slim, chunks, room):
    length = key_rows.shape[0]
    part = slim // chunks
    block = pl.BlockSpec((length, LANES), lambda i, me_ref: (0, jnp.bitwise_xor(me_ref[0] // group, t)))
    spec = pl.BlockSpec((2 * part, length), lambda i, me_ref: (0, 0))
    count = group * chunks
    return call(
        functools.partial(pack_body, group, slim, chunks),
        [jax.ShapeDtypeStruct((2 * part, length), f32)] * count,
        grid_spec=pltpu.PrefetchScalarGridSpec(
            num_scalar_prefetch=1,
            grid=(1,),
            in_specs=[block] * 3,
            out_specs=[spec] * count,
            scratch_shapes=[pltpu.VMEM((LANES, length), f32)] * 2,
        ),
        room=room,
    )(me, key_rows, value_rows, filters)


def spectrum_body(*refs):
    arrived, (fwd_high, fwd_low), out = refs[:-3], refs[-3:-1], refs[-1]
    rows = jnp.concatenate([ref[...] for ref in arrived], axis=0)
    high, low = halves(rows)
    out[...] = dot_split(high, low, fwd_high[...], fwd_low[...])


def spectrum(arrived, forward):
    double, length = arrived[0].shape
    vmem = pl.BlockSpec(memory_space=pltpu.VMEM)
    return call(
        spectrum_body,
        jax.ShapeDtypeStruct((len(arrived) * double, 2 * length), f32),
        in_specs=[vmem] * (2 + len(arrived)),
        out_specs=vmem,
        room=16,
    )(*arrived, *forward)


def products(count, part, length, spectra, totals):
    lane_steps = length // LANES

    def tile(index, carry):
        group = index // lane_steps
        lane = lax.rem(index, lane_steps)
        sign = jnp.where(lane * 2 < lane_steps, 1.0, -1.0).astype(f32)
        top = pl.ds(pl.multiple_of(group * 8, 8), 8)
        bottom = pl.ds(pl.multiple_of(part + group * 8, 8), 8)
        re = pl.ds(pl.multiple_of(lane * LANES, LANES), LANES)
        im = pl.ds(pl.multiple_of(length + lane * LANES, LANES), LANES)
        gated_re = [spectra[p, top, re] for p in range(count)]
        gated_im = [spectra[p, top, im] for p in range(count)]
        taps_re, taps_im = [], []
        last_re = last_im = None
        for q in range(count):
            now_re, now_im = spectra[q, bottom, re], spectra[q, bottom, im]
            if q == 0:
                taps_re.append(now_re)
                taps_im.append(now_im)
            else:
                taps_re.append(now_re - sign * last_im)
                taps_im.append(now_im + sign * last_re)
            last_re, last_im = now_re, now_im
        for i in range(count):
            total_re = total_im = None
            for p in range(i + 1):
                a_re, a_im = gated_re[p], gated_im[p]
                b_re, b_im = taps_re[i - p], taps_im[i - p]
                one_re = a_re * b_re - a_im * b_im
                one_im = a_re * b_im + a_im * b_re
                total_re = one_re if p == 0 else total_re + one_re
                total_im = one_im if p == 0 else total_im + one_im
            totals[i, top, re] = total_re
            totals[i, top, im] = total_im
        return carry

    lax.fori_loop(0, part // 8 * lane_steps, tile, 0)


def conv_body(early, late, me_ref, fwd_high, fwd_low, inv_high, inv_low, near, *rest):
    arrived = rest[: len(late)]
    outs = rest[len(late) : 2 * len(late)]
    left, spectra, totals = rest[2 * len(late) :]
    count = len(early) + len(late)
    me = me_ref[0]
    double, length = arrived[0].shape
    part = double // 2
    for e, s in enumerate(early):
        spectra[jnp.bitwise_xor(me, s)] = near[e * double : (e + 1) * double, :]
    rows = jnp.concatenate([ref[...] for ref in arrived], axis=0)
    high, low = halves(rows)
    result = dot_split(high, low, fwd_high[...], fwd_low[...])
    for e, s in enumerate(late):
        spectra[jnp.bitwise_xor(me, s)] = result[e * double : (e + 1) * double]
    products(count, part, length, spectra, totals)
    stacked = jnp.concatenate([totals[jnp.bitwise_xor(me, s)] for s in late], axis=0)
    high, low = halves(stacked)
    result = dot_split(high, low, inv_high[...], inv_low[...])
    for e in range(len(late)):
        outs[e][...] = result[e * part : (e + 1) * part]
    for e, s in enumerate(early):
        left[e * part : (e + 1) * part, :] = totals[jnp.bitwise_xor(me, s)]


def convolve(me, early, late, near, arrived, forward, inverse):
    count = len(early) + len(late)
    double, length = arrived[0].shape
    part = double // 2
    vmem = pl.BlockSpec(memory_space=pltpu.VMEM)
    return call(
        functools.partial(conv_body, early, late),
        [jax.ShapeDtypeStruct((part, length), f32)] * len(late)
        + [jax.ShapeDtypeStruct((len(early) * part, 2 * length), f32)],
        in_specs=[pl.BlockSpec(memory_space=pltpu.SMEM)] + [vmem] * (5 + len(late)),
        out_specs=[vmem] * (len(late) + 1),
        scratch=[
            pltpu.VMEM((count, double, 2 * length), f32),
            pltpu.VMEM((count, part, 2 * length), f32),
        ],
        room=24,
    )(me, *forward, *inverse, near, *arrived)


def restore_body(left, inv_high, inv_low, *outs):
    part = outs[0].shape[0]
    high, low = halves(left[...])
    result = dot_split(high, low, inv_high[...], inv_low[...])
    for e, out in enumerate(outs):
        out[...] = result[e * part : (e + 1) * part]


def restore(left, inverse, pieces):
    rows, width = left.shape
    vmem = pl.BlockSpec(memory_space=pltpu.VMEM)
    return call(
        restore_body,
        [jax.ShapeDtypeStruct((rows // pieces, width // 2), f32)] * pieces,
        in_specs=[vmem] * 3,
        out_specs=[vmem] * pieces,
        room=16,
    )(left, *inverse)


def gates_body(count, chunks, me_ref, query_ref, key_ref, value_ref, skip_ref, gate_ref, direct_ref, gate_t, direct_t):
    query = query_ref[...]
    gate_t[...] = query.T
    direct_t[...] = (query * (skip_ref[...] * (key_ref[...] * value_ref[...]))).T
    slim = gate_t.shape[0] // count
    part = slim // chunks
    for k in range(chunks):
        for s in range(count):
            start = jnp.bitwise_xor(me_ref[0], s) * slim + k * part
            source = pl.ds(pl.multiple_of(start, 8), part)
            here = pl.ds((k * count + s) * part, part)
            gate_ref[here, :] = gate_t[source, :]
            direct_ref[here, :] = direct_t[source, :]


def gates(me, query_rows, key_rows, value_rows, skip_gain, count, chunks):
    length, channels = query_rows.shape
    vmem = pl.BlockSpec(memory_space=pltpu.VMEM)
    return call(
        functools.partial(gates_body, count, chunks),
        [jax.ShapeDtypeStruct((channels, length), f32)] * 2,
        in_specs=[pl.BlockSpec(memory_space=pltpu.SMEM)] + [vmem] * 4,
        out_specs=[vmem] * 2,
        scratch=[pltpu.VMEM((channels, length), f32)] * 2,
        room=16,
        work=10**12,
    )(me, query_rows, key_rows, value_rows, skip_gain[None, :])


def mix_body(*refs):
    count = (len(refs) - 1) // 3
    out = refs[-1]
    part = refs[0].shape[0]
    for e in range(count):
        out[e * part : (e + 1) * part, :] = refs[count + e][...] * refs[e][...] + refs[2 * count + e][...]


def mix(pieces, gate, direct, first):
    part, length = pieces[0].shape
    count = len(pieces)

    def rows(e):
        return pl.BlockSpec((part, length), lambda i: (first + e, 0))

    whole = pl.BlockSpec((part, length), lambda i: (0, 0))
    return call(
        mix_body,
        jax.ShapeDtypeStruct((count * part, length), f32),
        grid_spec=pl.GridSpec(
            grid=(1,),
            in_specs=[whole] * count + [rows(e) for e in range(count)] * 2,
            out_specs=pl.BlockSpec((count * part, length), lambda i: (0, 0)),
        ),
        room=16,
    )(*pieces, *[gate] * count, *[direct] * count)


def cut_body(weight_ref, out_ref):
    out_ref[0] = weight_ref[...]


def cut(out_weight, peers):
    channels, total = out_weight.shape
    width = total // peers
    return call(
        cut_body,
        jax.ShapeDtypeStruct((peers, channels, width), f32),
        grid_spec=pl.GridSpec(
            grid=(peers,),
            in_specs=[pl.BlockSpec((channels, width), lambda o: (0, o))],
            out_specs=pl.BlockSpec((1, channels, width), lambda o: (o, 0, 0)),
        ),
        room=56,
    )(out_weight)


def weights_body(count, chunks, me_ref, mine_ref, weight_ref, high_ref, low_ref, ordered):
    slim = ordered.shape[0] // count
    part = slim // chunks
    for k in range(chunks):
        for s in range(count):
            start = jnp.bitwise_xor(me_ref[0], s) * slim + k * part
            ordered[pl.ds((k * count + s) * part, part), :] = weight_ref[0, pl.ds(pl.multiple_of(start, 8), part), :]
    high, low = halves(ordered[...].T)
    high_ref[...] = high
    low_ref[...] = low


def weights(me, mine, blocks, count, chunks):
    peers, channels, width = blocks.shape
    result = pl.BlockSpec((width, channels), lambda o, me_ref, mine_ref: (0, o))
    return call(
        functools.partial(weights_body, count, chunks),
        [jax.ShapeDtypeStruct((width, peers * channels), bf16)] * 2,
        grid_spec=pltpu.PrefetchScalarGridSpec(
            num_scalar_prefetch=2,
            grid=(peers,),
            in_specs=[pl.BlockSpec((1, channels, width), lambda o, me_ref, mine_ref: (jnp.bitwise_xor(mine_ref[0], o), 0, 0))],
            out_specs=[result] * 2,
            scratch_shapes=[pltpu.VMEM((channels, width), f32)],
        ),
        room=12,
        work=10**12,
    )(me, mine, blocks)


def project_body(count, started, *refs):
    mixed, highs, lows = refs[:count], refs[count : 2 * count], refs[2 * count : 3 * count]
    out = refs[-1]
    rows = jnp.concatenate([ref[...] for ref in mixed], axis=0)
    high, low = halves(rows)
    w_high = jnp.concatenate([ref[...] for ref in highs], axis=1)
    w_low = jnp.concatenate([ref[...] for ref in lows], axis=1)
    total = dot_split(w_high, w_low, high, low)
    if started:
        total = total + refs[3 * count][...]
    out[...] = total


def project(have, part, tables, peers, first, total):
    count = len(part)
    depth, length = have[0].shape
    high, low = tables
    width, columns = high.shape
    steps = columns // peers // depth
    whole = pl.BlockSpec((depth, length), lambda i: (0, 0))
    result = pl.BlockSpec((width, length), lambda i: (0, 0))

    def cut(o):
        return pl.BlockSpec((width, depth), lambda i: (0, o * steps + first))

    started = total is not None
    return call(
        functools.partial(project_body, count, started),
        jax.ShapeDtypeStruct((width, length), f32),
        grid_spec=pl.GridSpec(
            grid=(1,),
            in_specs=[whole] * count + [cut(o) for o in part] * 2 + [result] * started,
            out_specs=result,
        ),
        room=20,
        aliases={3 * count: 0} if started else None,
    )(*[have[o] for o in part], *[high] * count, *[low] * count, *([total] * started))


def swap(x, axis, size, offset):
    return lax.ppermute(x, axis, [(j, j ^ offset) for j in range(size)])


def gather(rows, peers, unit, tables, total, final):
    have = {0: rows}
    bit = peers // 2
    for o in range(1, bit):
        have[o] = swap(rows if o & (o - 1) == 0 else have[o & (o - 1)], "ch", peers, o & -o)
    far = swap(rows, "ch", peers, bit)
    if final:
        total = project(have, range(bit), tables, peers, unit, total)
        far, total = lax.optimization_barrier((far, total))
    have[bit] = far
    for o in range(1, bit):
        have[bit | o] = swap(far if o & (o - 1) == 0 else have[bit | (o & (o - 1))], "ch", peers, o & -o)
    if final:
        total = project(have, (bit,), tables, peers, unit, total)
        total = project(have, range(bit + 1, peers), tables, peers, unit, total)
    else:
        total = project(have, range(peers), tables, peers, unit, total)
    return total


def after(value, others):
    return lax.optimization_barrier((value, others))[0]


def per_device(query_rows, key_rows, value_rows, filters, skip_gain, out_weight):
    count = lax.axis_size("seq")
    peers = lax.axis_size("ch")
    length, channels = query_rows.shape
    slim = channels // count
    chunks = max(1, min(CHUNKS, slim // 8))
    group = LANES // slim
    width = out_weight.shape[1] // peers
    me = lax.axis_index("seq").astype(jnp.int32).reshape(1)
    mine = lax.axis_index("ch").astype(jnp.int32)
    forward, inverse = transforms(length)

    def pack_group(t, ready):
        pieces = pack(ready, key_rows, value_rows, filters, t, group, slim, chunks, 56 if t >= count // group // 2 else 8)
        for e in range(group):
            for k in range(chunks):
                sent[k][t * group + e] = pieces[e * chunks + k]
        return after(me, pieces)

    sent = [[None] * count for _ in range(chunks)]
    ready = me
    groups = count // group
    for t in list(range(groups // 2, groups)) + list(range(groups // 2)):
        ready = pack_group(t, ready)
    early, late = list(range(count // 2)), list(range(count // 2, count))
    arrived = [[None] * count for _ in range(chunks)]
    for k in range(chunks):
        for s in late + early:
            arrived[k][s] = swap(sent[k][s], "seq", count, s) if s else sent[k][0]
    blocks = cut(after(out_weight, ready), peers)
    blocks = lax.all_to_all(blocks, "ch", split_axis=0, concat_axis=0, tiled=True)
    gate, direct = gates(me, query_rows, key_rows, value_rows, skip_gain, count, chunks)

    total = None
    tables = None
    for k in range(chunks):
        near = spectrum([arrived[k][s] for s in early], forward)
        far = [arrived[k][s] for s in late]
        far, near, gate, direct = lax.optimization_barrier((far, near, gate, direct))
        back = [None] * count
        *pieces, left = convolve(me, early, late, near, far, forward, inverse)
        for s, piece in zip(late, pieces):
            back[s] = swap(piece, "seq", count, s)
        for s, piece in zip(early, restore(left, inverse, len(early))):
            back[s] = swap(piece, "seq", count, s) if s else piece
        if tables is None:
            tables = weights(after(me, left), mine.reshape(1), blocks, count, chunks)
        for u, unit in enumerate((early, late)):
            pieces = [back[s] for s in unit]
            if u:
                pieces, tables = lax.optimization_barrier((pieces, tables))
            rows = mix(pieces, gate, direct, k * count + unit[0])
            final = u and k == chunks - 1
            total = gather(rows, peers, k * 2 + u, tables, total, final)
    return total


def solution(mesh):
    in_specs = (
        P("seq", "ch"),
        P("seq", "ch"),
        P("seq", "ch"),
        P("seq", "ch"),
        P("ch"),
        P("ch", None),
    )
    out_specs = P("ch", "seq")
    return jax.shard_map(
        per_device, mesh=mesh, in_specs=in_specs, out_specs=out_specs, check_vma=False
    )
```

profile of v0, /device:TPU:9, one launch (start us, length us, event | category | flops | bytes accessed | tf_op | source)
XLA Modules:
  0.0 114.1 jit_solution(13065529017207947513)
XLA Ops:
  0.0 2.4 %shard_map.100 = (f32[128,512]{1,0:T(8,128)}, f32[128,512]{1,0:T(8,128)}) custom-call(s32[1]{0:T(128)} %bitcast.me_ref, f32[512,512]{1,0:T(8,128)} %key_ref.9, f32[512,512]{1,0:T(8,128)} %value_ref.9, f32[512,512]{1,0:T(8,128)} %filter_ref.7), custom_call_target="tpu_custom_call" | custom-call | flops 1 | bytes 1 | tf_op jit(solution)/shard_map/pallas_call | solution.py:79
  2.4 2.2 %shard_map.101 = (f32[128,512]{1,0:T(8,128)}, f32[128,512]{1,0:T(8,128)}) custom-call(s32[1]{0:T(128)} %bitcast.me_ref, f32[512,512]{1,0:T(8,128)} %key_ref.9, f32[512,512]{1,0:T(8,128)} %value_ref.9, f32[512,512]{1,0:T(8,128)} %filter_ref.7), custom_call_target="tpu_custom_call" | custom-call | flops 1 | bytes 1 | tf_op jit(solution)/shard_map/pallas_call | solution.py:79
  4.5 1.0 shard_map.102
  5.5 1.3 %collective-permute-start.4 = (f32[128,512]{1,0:T(8,128)}, f32[128,512]{1,0:T(8,128)}, u32[]{:S(2)}, u32[]{:S(2)}) collective-permute-start(f32[128,512]{1,0:T(8,128)} %get-tuple-element.52), channel_id=1, source_target_pairs={{0,4},{4,0},{8,12},{12,8},{16,20},{20,16},{24,28},{28,24},{1,5},{5... | collective-permute-start | bytes 786440 | tf_op jit(solution)/shard_map/ppermute | solution.py:362
  6.8 1.1 shard_map.103
  7.9 0.2 collective-permute-start.5
  8.0 2.3 %collective-permute-start = (f32[128,512]{1,0:T(8,128)}, f32[128,512]{1,0:T(8,128)}, u32[]{:S(2)}, u32[]{:S(2)}) collective-permute-start(f32[128,512]{1,0:T(8,128)} %get-tuple-element.45), channel_id=1, source_target_pairs={{0,16},{4,20},{8,24},{12,28},{16,0},{20,4},{24,8},{28,12},{1,17},{... | collective-permute-start | bytes 786440 | tf_op jit(solution)/shard_map/ppermute | solution.py:362
  10.3 2.4 %collective-permute-start.2 = (f32[128,512]{1,0:T(8,128)}, f32[128,512]{1,0:T(8,128)}, u32[]{:S(2)}, u32[]{:S(2)}) collective-permute-start(f32[128,512]{1,0:T(8,128)} %get-tuple-element.48), channel_id=1, source_target_pairs={{0,24},{4,28},{8,16},{12,20},{16,8},{20,12},{24,0},{28,4},{1,25},{... | collective-permute-start | bytes 786440 | tf_op jit(solution)/shard_map/ppermute | solution.py:362
  12.8 4.8 %shard_map.107 = f32[4,512,512]{2,1,0:T(8,128)} custom-call(f32[512,2048]{1,0:T(8,128)} %weight_ref), custom_call_target="tpu_custom_call" | custom-call | flops 1 | bytes 1 | tf_op jit(solution)/shard_map/pallas_call | solution.py:280
  17.6 7.0 %all-to-all-start = ((f32[4,512,512]{2,1,0:T(8,128)}), f32[4,512,512]{2,1,0:T(8,128)}, u32[]{:S(2)}, u32[]{:S(2)}) async-start(f32[4,512,512]{2,1,0:T(8,128)} %shard_map.107), calls=%async_computation | async-start | bytes 8388608 | tf_op jit(solution)/shard_map/all_to_all | solution.py:419
  24.6 0.7 collective-permute-start.3
  25.3 0.0 collective-permute-done.5.refs_2_
  25.3 0.7 copy-done.8
  26.0 2.3 %collective-permute-start.6 = (f32[128,512]{1,0:T(8,128)}, f32[128,512]{1,0:T(8,128)}, u32[]{:S(2)}, u32[]{:S(2)}) collective-permute-start(f32[128,512]{1,0:T(8,128)} %get-tuple-element.55), channel_id=1, source_target_pairs={{0,12},{4,8},{8,4},{12,0},{16,28},{20,24},{24,20},{28,16},{1,13},{... | collective-permute-start | bytes 786440 | tf_op jit(solution)/shard_map/ppermute | solution.py:362
  28.4 1.2 %copy-done.3 = f32[512,512]{1,0:T(8,128)S(1)} copy-done((f32[512,512]{1,0:T(8,128)S(1)}, f32[512,512]{1,0:T(8,128)}, u32[]{:S(2)}) %copy-start.3) | copy-done | bytes 1048600
  29.6 1.2 %copy-done.10 = f32[512,512]{1,0:T(8,128)S(1)} copy-done((f32[512,512]{1,0:T(8,128)S(1)}, f32[512,512]{1,0:T(8,128)}, u32[]{:S(2)}) %copy-start.10) | copy-done | bytes 1048600
  30.8 0.7 shard_map.105
  31.5 0.0 copy-start.4
  31.5 0.0 copy-start.5
  31.6 18.6 %collective-permute-done.6.refs_3_ = f32[128,512]{1,0:T(8,128)} collective-permute-done((f32[128,512]{1,0:T(8,128)}, f32[128,512]{1,0:T(8,128)}, u32[]{:S(2)}, u32[]{:S(2)}) %collective-permute-start.6) | collective-permute-done | bytes 262176 | tf_op jit(solution)/shard_map/ppermute | solution.py:362
  50.2 2.8 %shard_map.104.near = f32[512,1024]{1,0:T(8,128)S(1)} custom-call(f32[128,512]{1,0:T(8,128)S(1)} %get-tuple-element.51.refs_0_, f32[128,512]{1,0:T(8,128)} %collective-permute-done.4.refs_1_, f32[128,512]{1,0:T(8,128)S(1)} %copy-done.9, f32[128,512]{1,0:T(8,128)} %collective-permute-done.6.refs_3_, bf16[512,1024]{1,0:T(8,128)(2,1)S(1)} %copy-done.6, ...), custom_call_target="tpu_custom_call" | custom-call | flops 1 | bytes 1 | tf_op jit(solution)/shard_map/pallas_call | solution.py:103
  53.0 0.0 collective-permute-done.1.rest_1_
  53.1 2.3 %collective-permute-done.3.rest_3_ = f32[128,512]{1,0:T(8,128)} collective-permute-done((f32[128,512]{1,0:T(8,128)}, f32[128,512]{1,0:T(8,128)}, u32[]{:S(2)}, u32[]{:S(2)}) %collective-permute-start.3) | collective-permute-done | bytes 262176 | tf_op jit(solution)/shard_map/ppermute | solution.py:362
  55.3 6.7 %shard_map.106 = (f32[64,512]{1,0:T(8,128)}, f32[64,512]{1,0:T(8,128)}, f32[64,512]{1,0:T(8,128)}, f32[64,512]{1,0:T(8,128)}, f32[256,1024]{1,0:T(8,128)S(1)}) custom-call(s32[1]{0:T(128)} %bitcast.me_ref, bf16[512,1024]{1,0:T(8,128)(2,1)S(1)} %copy-done.6, bf16[512,1024]{1,0:T(8,128)(2,1)S(1)} %copy-done.7, bf16[1024,512]{1,0:T(8,128)(2,1)S(1)} %copy-done.4, ...), custom_call_target="tpu_custom_call" | custom-call | flops 1 | bytes 1 | tf_op jit(solution)/shard_map/pallas_call | solution.py:182
  62.0 1.0 shard_map.110
  63.0 1.3 %collective-permute-start.13 = (f32[64,512]{1,0:T(8,128)S(1)}, f32[64,512]{1,0:T(8,128)S(1)}, u32[]{:S(2)}, u32[]{:S(2)}) collective-permute-start(f32[64,512]{1,0:T(8,128)S(1)} %get-tuple-element.80), channel_id=1, source_target_pairs={{0,4},{4,0},{8,12},{12,8},{16,20},{20,16},{24,28},{28,24},{1,5},{5... | collective-permute-start | bytes 393224 | tf_op jit(solution)/shard_map/ppermute | solution.py:362
  64.3 0.0 collective-permute-start.14
  64.3 1.4 %collective-permute-start.15 = (f32[64,512]{1,0:T(8,128)S(1)}, f32[64,512]{1,0:T(8,128)S(1)}, u32[]{:S(2)}, u32[]{:S(2)}) collective-permute-start(f32[64,512]{1,0:T(8,128)S(1)} %get-tuple-element.82), channel_id=1, source_target_pairs={{0,12},{4,8},{8,4},{12,0},{16,28},{20,24},{24,20},{28,16},{1,13},{... | collective-permute-start | bytes 393224 | tf_op jit(solution)/shard_map/ppermute | solution.py:362
  65.7 1.1 collective-permute-start.7
  66.8 2.3 %collective-permute-start.8 = (f32[64,512]{1,0:T(8,128)}, f32[64,512]{1,0:T(8,128)}, u32[]{:S(2)}, u32[]{:S(2)}) collective-permute-start(f32[64,512]{1,0:T(8,128)} %get-tuple-element.64), channel_id=1, source_target_pairs={{0,20},{4,16},{8,28},{12,24},{16,4},{20,0},{24,12},{28,8},{1,21},{... | collective-permute-start | bytes 393224 | tf_op jit(solution)/shard_map/ppermute | solution.py:362
  69.1 1.3 %collective-permute-start.9 = (f32[64,512]{1,0:T(8,128)}, f32[64,512]{1,0:T(8,128)}, u32[]{:S(2)}, u32[]{:S(2)}) collective-permute-start(f32[64,512]{1,0:T(8,128)} %get-tuple-element.65), channel_id=1, source_target_pairs={{0,24},{4,28},{8,16},{12,20},{16,8},{20,12},{24,0},{28,4},{1,25},{... | collective-permute-start | bytes 393224 | tf_op jit(solution)/shard_map/ppermute | solution.py:362
  70.4 0.1 collective-permute-start.10
  70.5 0.9 shard_map.111.refs_0_
  71.4 1.2 %collective-permute-start.17 = (f32[256,512]{1,0:T(8,128)}, f32[256,512]{1,0:T(8,128)}, u32[]{:S(2)}, u32[]{:S(2)}) collective-permute-start(f32[256,512]{1,0:T(8,128)} %shard_map.111.refs_0_), channel_id=1, source_target_pairs={{0,2},{1,3},{2,0},{3,1},{4,6},{5,7},{6,4},{7,5},{8,10},{9,11},{10,... | collective-permute-start | bytes 1572872 | tf_op jit(solution)/shard_map/ppermute | solution.py:362
  72.6 3.8 %shard_map.108 = (bf16[512,2048]{1,0:T(8,128)(2,1)S(1)}, bf16[512,2048]{1,0:T(8,128)(2,1)S(1)}) custom-call(s32[1]{0:T(128)} %bitcast.me_ref, s32[1]{0:T(128)} %bitcast.2.mine_ref, f32[4,512,512]{2,1,0:T(8,128)} %all-to-all-done.weight_ref), custom_call_target="tpu_custom_call" | custom-call | flops 999999995904 | bytes 1 | tf_op jit(solution)/shard_map/pallas_call | solution.py:307
  76.5 7.8 %collective-permute-start.16 = (f32[256,512]{1,0:T(8,128)}, f32[256,512]{1,0:T(8,128)S(1)}, u32[]{:S(2)}, u32[]{:S(2)}) collective-permute-start(f32[256,512]{1,0:T(8,128)} %shard_map.111.refs_0_), channel_id=1, source_target_pairs={{0,1},{1,0},{2,3},{3,2},{4,5},{5,4},{6,7},{7,6},{8,9},{9,8},{10,11... | collective-permute-start | bytes 1572872 | tf_op jit(solution)/shard_map/ppermute | solution.py:362
  84.3 1.8 %collective-permute-start.18 = (f32[256,512]{1,0:T(8,128)}, f32[256,512]{1,0:T(8,128)S(1)}, u32[]{:S(2)}, u32[]{:S(2)}) collective-permute-start(f32[256,512]{1,0:T(8,128)} %collective-permute-done.17.refs_2_), channel_id=1, source_target_pairs={{0,1},{1,0},{2,3},{3,2},{4,5},{5,4},{6,7},{7,6},{8,9},{9,8},{10,11... | collective-permute-start | bytes 1572872 | tf_op jit(solution)/shard_map/ppermute | solution.py:362
  86.1 2.2 %collective-permute-done.9.refs_2_ = f32[64,512]{1,0:T(8,128)} collective-permute-done((f32[64,512]{1,0:T(8,128)}, f32[64,512]{1,0:T(8,128)}, u32[]{:S(2)}, u32[]{:S(2)}) %collective-permute-start.9) | collective-permute-done | bytes 131104 | tf_op jit(solution)/shard_map/ppermute | solution.py:362
  88.3 2.0 %collective-permute-done.10.refs_3_ = f32[64,512]{1,0:T(8,128)} collective-permute-done((f32[64,512]{1,0:T(8,128)}, f32[64,512]{1,0:T(8,128)}, u32[]{:S(2)}, u32[]{:S(2)}) %collective-permute-start.10) | collective-permute-done | bytes 131104 | tf_op jit(solution)/shard_map/ppermute | solution.py:362
  90.3 1.2 %shard_map.109.refs_0_ = f32[256,512]{1,0:T(8,128)S(1)} custom-call(f32[64,512]{1,0:T(8,128)} %collective-permute-done.7.refs_0_, f32[64,512]{1,0:T(8,128)} %collective-permute-done.8.refs_1_, f32[64,512]{1,0:T(8,128)} %collective-permute-done.9.refs_2_, f32[64,512]{1,0:T(8,128)} %collective-permute-done.10.refs_3_, ...), custom_call_target="tpu_custom_call" | custom-call | flops 1 | bytes 1 | tf_op jit(solution)/shard_map/pallas_call | solution.py:261
  91.5 2.6 %collective-permute-start.12 = (f32[256,512]{1,0:T(8,128)S(1)}, f32[256,512]{1,0:T(8,128)S(1)}, u32[]{:S(2)}, u32[]{:S(2)}) collective-permute-start(f32[256,512]{1,0:T(8,128)S(1)} %shard_map.109.refs_0_), channel_id=1, source_target_pairs={{0,1},{1,0},{2,3},{3,2},{4,5},{5,4},{6,7},{7,6},{8,9},{9,8},{10,11... | collective-permute-start | bytes 1572872 | tf_op jit(solution)/shard_map/ppermute | solution.py:362
  94.1 1.2 %collective-permute-start.11 = (f32[256,512]{1,0:T(8,128)S(1)}, f32[256,512]{1,0:T(8,128)S(1)}, u32[]{:S(2)}, u32[]{:S(2)}) collective-permute-start(f32[256,512]{1,0:T(8,128)S(1)} %shard_map.109.refs_0_), channel_id=1, source_target_pairs={{0,2},{1,3},{2,0},{3,1},{4,6},{5,7},{6,4},{7,5},{8,10},{9,11},{10,... | collective-permute-start | bytes 1572872 | tf_op jit(solution)/shard_map/ppermute | solution.py:362
  95.3 4.0 %shard_map.112.refs_6_ = f32[512,512]{1,0:T(8,128)} custom-call(f32[256,512]{1,0:T(8,128)} %shard_map.111.refs_0_, f32[256,512]{1,0:T(8,128)S(1)} %collective-permute-done.16.refs_1_, f32[256,512]{1,0:T(8,128)} %collective-permute-done.17.refs_2_, f32[256,512]{1,0:T(8,128)S(1)} %collective-permute-done.18.refs_3_, ...), custom_call_target="tpu_custom_call" | custom-call | flops 1 | bytes 1 | tf_op jit(solution)/shard_map/pallas_call | solution.py:348
  99.3 3.3 %shard_map.113.refs_3_ = f32[512,512]{1,0:T(8,128)} custom-call(f32[256,512]{1,0:T(8,128)S(1)} %shard_map.109.refs_0_, f32[256,512]{1,0:T(8,128)S(1)} %collective-permute-done.12.refs_1_, bf16[512,2048]{1,0:T(8,128)(2,1)S(1)} %get-tuple-element.77.refs_4_.refs_5_.refs_6_.refs_7_.refs_2_.refs_3_.refs_1_, ...), custom_call_target="tpu_custom_call", output_to_operand_aliasing={{}: (6, {})} | custom-call | flops 1 | bytes 1 | tf_op jit(solution)/shard_map/pallas_call | solution.py:348
  102.6 4.9 %collective-permute-done.11.refs_0_ = f32[256,512]{1,0:T(8,128)S(1)} collective-permute-done((f32[256,512]{1,0:T(8,128)S(1)}, f32[256,512]{1,0:T(8,128)S(1)}, u32[]{:S(2)}, u32[]{:S(2)}) %collective-permute-start.11) | collective-permute-done | bytes 524320 | tf_op jit(solution)/shard_map/ppermute | solution.py:362
  107.6 0.8 collective-permute-start.19
  108.4 2.9 %shard_map.114.refs_3_ = f32[512,512]{1,0:T(8,128)} custom-call(f32[256,512]{1,0:T(8,128)S(1)} %collective-permute-done.11.refs_0_, bf16[512,2048]{1,0:T(8,128)(2,1)S(1)} %get-tuple-element.77.refs_4_.refs_5_.refs_6_.refs_7_.refs_2_.refs_3_.refs_1_, ...), custom_call_target="tpu_custom_call", output_to_operand_aliasing={{}: (3, {})} | custom-call | flops 1 | bytes 1 | tf_op jit(solution)/shard_map/pallas_call | solution.py:348
  111.3 2.9 %shard_map.115 = f32[512,512]{1,0:T(8,128)} custom-call(f32[256,512]{1,0:T(8,128)S(1)} %collective-permute-done.19.refs_0_, bf16[512,2048]{1,0:T(8,128)(2,1)S(1)} %get-tuple-element.77.refs_4_.refs_5_.refs_6_.refs_7_.refs_2_.refs_3_.refs_1_, ...), custom_call_target="tpu_custom_call", output_to_operand_aliasing={{}: (3, {})} | custom-call | flops 1 | bytes 1 | tf_op jit(solution)/shard_map/pallas_call | solution.py:348
  (34 shorter events, 0.1 us)
Async XLA Ops:
  0.0 4.5 %copy-start.1 = (f32[512,512]{1,0:T(8,128)S(1)}, f32[512,512]{1,0:T(8,128)}, u32[]{:S(2)}) copy-start(f32[512,512]{1,0:T(8,128)} %key_ref.9) | copy-start | bytes 3145732
  0.0 4.5 %copy-start.2 = (f32[512,512]{1,0:T(8,128)S(1)}, f32[512,512]{1,0:T(8,128)}, u32[]{:S(2)}) copy-start(f32[512,512]{1,0:T(8,128)} %value_ref.9) | copy-start | bytes 3145732
  0.0 4.5 %copy-start = (f32[512,512]{1,0:T(8,128)S(1)}, f32[512,512]{1,0:T(8,128)}, u32[]{:S(2)}) copy-start(f32[512,512]{1,0:T(8,128)} %filter_ref.7) | copy-start | bytes 3145732
  5.5 19.1 %collective-permute-start.4 = (f32[128,512]{1,0:T(8,128)}, f32[128,512]{1,0:T(8,128)}, u32[]{:S(2)}, u32[]{:S(2)}) collective-permute-start(f32[128,512]{1,0:T(8,128)} %get-tuple-element.52), channel_id=1, source_target_pairs={{0,4},{4,0},{8,12},{12,8},{16,20},{20,16},{24,28},{28,24},{1,5},{5... | collective-permute-start | bytes 786440 | tf_op jit(solution)/shard_map/ppermute | solution.py:362
  7.9 17.4 %collective-permute-start.5 = (f32[128,512]{1,0:T(8,128)}, f32[128,512]{1,0:T(8,128)S(1)}, u32[]{:S(2)}, u32[]{:S(2)}) collective-permute-start(f32[128,512]{1,0:T(8,128)} %get-tuple-element.54), channel_id=1, source_target_pairs={{0,8},{4,12},{8,0},{12,4},{16,24},{20,28},{24,16},{28,20},{1,9},{5... | collective-permute-start | bytes 786440 | tf_op jit(solution)/shard_map/ppermute | solution.py:362
  8.0 45.0 %collective-permute-start = (f32[128,512]{1,0:T(8,128)}, f32[128,512]{1,0:T(8,128)}, u32[]{:S(2)}, u32[]{:S(2)}) collective-permute-start(f32[128,512]{1,0:T(8,128)} %get-tuple-element.45), channel_id=1, source_target_pairs={{0,16},{4,20},{8,24},{12,28},{16,0},{20,4},{24,8},{28,12},{1,17},{... | collective-permute-start | bytes 786440 | tf_op jit(solution)/shard_map/ppermute | solution.py:362
  10.3 42.7 %collective-permute-start.1 = (f32[128,512]{1,0:T(8,128)}, f32[128,512]{1,0:T(8,128)}, u32[]{:S(2)}, u32[]{:S(2)}) collective-permute-start(f32[128,512]{1,0:T(8,128)} %get-tuple-element.46), channel_id=1, source_target_pairs={{0,20},{4,16},{8,28},{12,24},{16,4},{20,0},{24,12},{28,8},{1,21},{... | collective-permute-start | bytes 786440 | tf_op jit(solution)/shard_map/ppermute | solution.py:362
  10.3 42.7 %collective-permute-start.2 = (f32[128,512]{1,0:T(8,128)}, f32[128,512]{1,0:T(8,128)}, u32[]{:S(2)}, u32[]{:S(2)}) collective-permute-start(f32[128,512]{1,0:T(8,128)} %get-tuple-element.48), channel_id=1, source_target_pairs={{0,24},{4,28},{8,16},{12,20},{16,8},{20,12},{24,0},{28,4},{1,25},{... | collective-permute-start | bytes 786440 | tf_op jit(solution)/shard_map/ppermute | solution.py:362
  17.6 10.8 %copy-start.11 = (f32[512]{0:T(512)S(1)}, f32[512]{0:T(512)}, u32[]{:S(2)}) copy-start(f32[512]{0:T(512)} %param.14) | copy-start | bytes 6148
  17.6 55.0 %all-to-all-start = ((f32[4,512,512]{2,1,0:T(8,128)}), f32[4,512,512]{2,1,0:T(8,128)}, u32[]{:S(2)}, u32[]{:S(2)}) async-start(f32[4,512,512]{2,1,0:T(8,128)} %shard_map.107), calls=%async_computation | async-start | bytes 8388608 | tf_op jit(solution)/shard_map/all_to_all | solution.py:419
  24.6 30.7 %collective-permute-start.3 = (f32[128,512]{1,0:T(8,128)}, f32[128,512]{1,0:T(8,128)}, u32[]{:S(2)}, u32[]{:S(2)}) collective-permute-start(f32[128,512]{1,0:T(8,128)} %get-tuple-element.49), channel_id=1, source_target_pairs={{0,28},{4,24},{8,20},{12,16},{16,12},{20,8},{24,4},{28,0},{1,29},{... | collective-permute-start | bytes 786440 | tf_op jit(solution)/shard_map/ppermute | solution.py:362
  25.3 0.7 copy-start.8
  26.0 24.2 %collective-permute-start.6 = (f32[128,512]{1,0:T(8,128)}, f32[128,512]{1,0:T(8,128)}, u32[]{:S(2)}, u32[]{:S(2)}) collective-permute-start(f32[128,512]{1,0:T(8,128)} %get-tuple-element.55), channel_id=1, source_target_pairs={{0,12},{4,8},{8,4},{12,0},{16,28},{20,24},{24,20},{28,16},{1,13},{... | collective-permute-start | bytes 786440 | tf_op jit(solution)/shard_map/ppermute | solution.py:362
  28.4 1.2 %copy-start.3 = (f32[512,512]{1,0:T(8,128)S(1)}, f32[512,512]{1,0:T(8,128)}, u32[]{:S(2)}) copy-start(f32[512,512]{1,0:T(8,128)} %value_ref.9) | copy-start | bytes 3145732
  29.6 1.2 %copy-start.10 = (f32[512,512]{1,0:T(8,128)S(1)}, f32[512,512]{1,0:T(8,128)}, u32[]{:S(2)}) copy-start(f32[512,512]{1,0:T(8,128)} %query_ref.1) | copy-start | bytes 3145732
  30.8 19.4 %copy-start.6 = (bf16[512,1024]{1,0:T(8,128)(2,1)S(1)}, bf16[512,1024]{1,0:T(8,128)(2,1)}, u32[]{:S(2)}) copy-start(bf16[512,1024]{1,0:T(8,128)(2,1)} %constant.17.clone.refs_4_.fwd_high) | copy-start | bytes 3145732
  30.8 19.4 %copy-start.7 = (bf16[512,1024]{1,0:T(8,128)(2,1)S(1)}, bf16[512,1024]{1,0:T(8,128)(2,1)}, u32[]{:S(2)}) copy-start(bf16[512,1024]{1,0:T(8,128)(2,1)} %constant.18.clone.refs_5_.fwd_low) | copy-start | bytes 3145732
  30.8 19.4 %copy-start.9 = (f32[128,512]{1,0:T(8,128)S(1)}, f32[128,512]{1,0:T(8,128)}, u32[]{:S(2)}) copy-start(f32[128,512]{1,0:T(8,128)} %copy-done.8) | copy-start | bytes 786436
  31.5 23.8 %copy-start.4 = (bf16[1024,512]{1,0:T(8,128)(2,1)S(1)}, bf16[1024,512]{1,0:T(8,128)(2,1)}, u32[]{:S(2)}) copy-start(bf16[1024,512]{1,0:T(8,128)(2,1)} %constant.19.clone.inv_high) | copy-start | bytes 3145732
  31.5 23.8 %copy-start.5 = (bf16[1024,512]{1,0:T(8,128)(2,1)S(1)}, bf16[1024,512]{1,0:T(8,128)(2,1)}, u32[]{:S(2)}) copy-start(bf16[1024,512]{1,0:T(8,128)(2,1)} %constant.20.clone.inv_low) | copy-start | bytes 3145732
  63.0 6.0 %collective-permute-start.13 = (f32[64,512]{1,0:T(8,128)S(1)}, f32[64,512]{1,0:T(8,128)S(1)}, u32[]{:S(2)}, u32[]{:S(2)}) collective-permute-start(f32[64,512]{1,0:T(8,128)S(1)} %get-tuple-element.80), channel_id=1, source_target_pairs={{0,4},{4,0},{8,12},{12,8},{16,20},{20,16},{24,28},{28,24},{1,5},{5... | collective-permute-start | bytes 393224 | tf_op jit(solution)/shard_map/ppermute | solution.py:362
  64.3 6.0 %collective-permute-start.14 = (f32[64,512]{1,0:T(8,128)S(1)}, f32[64,512]{1,0:T(8,128)S(1)}, u32[]{:S(2)}, u32[]{:S(2)}) collective-permute-start(f32[64,512]{1,0:T(8,128)S(1)} %get-tuple-element.81), channel_id=1, source_target_pairs={{0,8},{4,12},{8,0},{12,4},{16,24},{20,28},{24,16},{28,20},{1,9},{5... | collective-permute-start | bytes 393224 | tf_op jit(solution)/shard_map/ppermute | solution.py:362
  64.3 6.1 %collective-permute-start.15 = (f32[64,512]{1,0:T(8,128)S(1)}, f32[64,512]{1,0:T(8,128)S(1)}, u32[]{:S(2)}, u32[]{:S(2)}) collective-permute-start(f32[64,512]{1,0:T(8,128)S(1)} %get-tuple-element.82), channel_id=1, source_target_pairs={{0,12},{4,8},{8,4},{12,0},{16,28},{20,24},{24,20},{28,16},{1,13},{... | collective-permute-start | bytes 393224 | tf_op jit(solution)/shard_map/ppermute | solution.py:362
  65.7 10.7 %collective-permute-start.7 = (f32[64,512]{1,0:T(8,128)}, f32[64,512]{1,0:T(8,128)}, u32[]{:S(2)}, u32[]{:S(2)}) collective-permute-start(f32[64,512]{1,0:T(8,128)} %get-tuple-element.63), channel_id=1, source_target_pairs={{0,16},{4,20},{8,24},{12,28},{16,0},{20,4},{24,8},{28,12},{1,17},{... | collective-permute-start | bytes 393224 | tf_op jit(solution)/shard_map/ppermute | solution.py:362
  66.8 19.2 %collective-permute-start.8 = (f32[64,512]{1,0:T(8,128)}, f32[64,512]{1,0:T(8,128)}, u32[]{:S(2)}, u32[]{:S(2)}) collective-permute-start(f32[64,512]{1,0:T(8,128)} %get-tuple-element.64), channel_id=1, source_target_pairs={{0,20},{4,16},{8,28},{12,24},{16,4},{20,0},{24,12},{28,8},{1,21},{... | collective-permute-start | bytes 393224 | tf_op jit(solution)/shard_map/ppermute | solution.py:362
  69.1 19.2 %collective-permute-start.9 = (f32[64,512]{1,0:T(8,128)}, f32[64,512]{1,0:T(8,128)}, u32[]{:S(2)}, u32[]{:S(2)}) collective-permute-start(f32[64,512]{1,0:T(8,128)} %get-tuple-element.65), channel_id=1, source_target_pairs={{0,24},{4,28},{8,16},{12,20},{16,8},{20,12},{24,0},{28,4},{1,25},{... | collective-permute-start | bytes 393224 | tf_op jit(solution)/shard_map/ppermute | solution.py:362
  70.4 20.0 %collective-permute-start.10 = (f32[64,512]{1,0:T(8,128)}, f32[64,512]{1,0:T(8,128)}, u32[]{:S(2)}, u32[]{:S(2)}) collective-permute-start(f32[64,512]{1,0:T(8,128)} %get-tuple-element.66), channel_id=1, source_target_pairs={{0,28},{4,24},{8,20},{12,16},{16,12},{20,8},{24,4},{28,0},{1,29},{... | collective-permute-start | bytes 393224 | tf_op jit(solution)/shard_map/ppermute | solution.py:362
  71.4 12.9 %collective-permute-start.17 = (f32[256,512]{1,0:T(8,128)}, f32[256,512]{1,0:T(8,128)}, u32[]{:S(2)}, u32[]{:S(2)}) collective-permute-start(f32[256,512]{1,0:T(8,128)} %shard_map.111.refs_0_), channel_id=1, source_target_pairs={{0,2},{1,3},{2,0},{3,1},{4,6},{5,7},{6,4},{7,5},{8,10},{9,11},{10,... | collective-permute-start | bytes 1572872 | tf_op jit(solution)/shard_map/ppermute | solution.py:362
  76.5 18.8 %collective-permute-start.16 = (f32[256,512]{1,0:T(8,128)}, f32[256,512]{1,0:T(8,128)S(1)}, u32[]{:S(2)}, u32[]{:S(2)}) collective-permute-start(f32[256,512]{1,0:T(8,128)} %shard_map.111.refs_0_), channel_id=1, source_target_pairs={{0,1},{1,0},{2,3},{3,2},{4,5},{5,4},{6,7},{7,6},{8,9},{9,8},{10,11... | collective-permute-start | bytes 1572872 | tf_op jit(solution)/shard_map/ppermute | solution.py:362
  84.3 11.1 %collective-permute-start.18 = (f32[256,512]{1,0:T(8,128)}, f32[256,512]{1,0:T(8,128)S(1)}, u32[]{:S(2)}, u32[]{:S(2)}) collective-permute-start(f32[256,512]{1,0:T(8,128)} %collective-permute-done.17.refs_2_), channel_id=1, source_target_pairs={{0,1},{1,0},{2,3},{3,2},{4,5},{5,4},{6,7},{7,6},{8,9},{9,8},{10,11... | collective-permute-start | bytes 1572872 | tf_op jit(solution)/shard_map/ppermute | solution.py:362
  91.5 7.8 %collective-permute-start.12 = (f32[256,512]{1,0:T(8,128)S(1)}, f32[256,512]{1,0:T(8,128)S(1)}, u32[]{:S(2)}, u32[]{:S(2)}) collective-permute-start(f32[256,512]{1,0:T(8,128)S(1)} %shard_map.109.refs_0_), channel_id=1, source_target_pairs={{0,1},{1,0},{2,3},{3,2},{4,5},{5,4},{6,7},{7,6},{8,9},{9,8},{10,11... | collective-permute-start | bytes 1572872 | tf_op jit(solution)/shard_map/ppermute | solution.py:362
  94.1 13.5 %collective-permute-start.11 = (f32[256,512]{1,0:T(8,128)S(1)}, f32[256,512]{1,0:T(8,128)S(1)}, u32[]{:S(2)}, u32[]{:S(2)}) collective-permute-start(f32[256,512]{1,0:T(8,128)S(1)} %shard_map.109.refs_0_), channel_id=1, source_target_pairs={{0,2},{1,3},{2,0},{3,1},{4,6},{5,7},{6,4},{7,5},{8,10},{9,11},{10,... | collective-permute-start | bytes 1572872 | tf_op jit(solution)/shard_map/ppermute | solution.py:362
  107.6 3.7 %collective-permute-start.19 = (f32[256,512]{1,0:T(8,128)S(1)}, f32[256,512]{1,0:T(8,128)S(1)}, u32[]{:S(2)}, u32[]{:S(2)}) collective-permute-start(f32[256,512]{1,0:T(8,128)S(1)} %collective-permute-done.11.refs_0_), channel_id=1, source_target_pairs={{0,1},{1,0},{2,3},{3,2},{4,5},{5,4},{6,7},{7,6},{8,9},{9,8},{10,11... | collective-permute-start | bytes 1572872 | tf_op jit(solution)/shard_map/ppermute | solution.py:362
where the time goes:
time: 115 us; the launch traced here: 114 us
  Pallas kernels  41.6 us (36%)
  starting transfers between devices  39.1 us (34%)
  waiting for transfers between devices  30.1 us (26%)
  local copies, waits for them, and re-layouts  3.19 us (3%)
    ppermute x20, starting transfers between devices, swap(): return lax.ppermute(x, axis, [(j, j ^ offset) for j in range(size)])  32.1 us
    ppermute x20, waiting for transfers between devices, swap(): return lax.ppermute(x, axis, [(j, j ^ offset) for j in range(size)])  30.1 us
    pallas_call x4, Pallas kernels, project(): call(functools.partial(project_body, count, started), jax.ShapeDtypeStruc...  13 us
    all_to_all x1, starting transfers between devices, per_device(): lax.all_to_all(blocks, 'ch', split_axis=0, concat_axis=0, tiled=True)  7.02 us
    pallas_call x1, Pallas kernels, convolve(): call(functools.partial(conv_body, early, late), [jax.ShapeDtypeStruct((pa...  6.73 us
    pallas_call x4, Pallas kernels, pack(): call(functools.partial(pack_body, group, slim, chunks), [jax.ShapeDtypeSt...  6.57 us
    pallas_call x1, Pallas kernels, cut(): call(cut_body, jax.ShapeDtypeStruct((peers, channels, width), f32), grid_...  4.83 us
    pallas_call x1, Pallas kernels, weights(): call(functools.partial(weights_body, count, chunks), [jax.ShapeDtypeStruc...  3.83 us
  transfers between devices with their start and end apart: 21, of which 5 were waited for; matrix products, arithmetic and copies ran while one was open for 0% of the time, Pallas kernels for 29%

commit v1 on v0

v1 whole, which is shorter than its diff:
```python
import functools
import math

import jax
import jax.numpy as jnp
import ml_dtypes
import numpy as np
from jax import lax
from jax.experimental import pallas as pl
from jax.experimental.pallas import tpu as pltpu
from jax.sharding import PartitionSpec as P

LANES = 128
MIB = 1024 * 1024
CHUNKS = 1

f32 = jnp.float32
bf16 = jnp.bfloat16


def halves(x):
    high = x.astype(bf16)
    return high, (x - high.astype(f32)).astype(bf16)


def dot(a, b):
    return jnp.dot(a, b, preferred_element_type=f32)


def dot_split(a_high, a_low, b_high, b_low):
    return dot(a_high, b_high) + (dot(a_low, b_high) + dot(a_high, b_low))


def split_table(table):
    high = table.astype(np.float32).astype(ml_dtypes.bfloat16)
    low = (table - high.astype(np.float64)).astype(np.float32).astype(ml_dtypes.bfloat16)
    return jnp.asarray(high), jnp.asarray(low)


def transforms(length):
    orders = np.concatenate([np.arange(0, length, 2), np.arange(1, length, 2)])
    angle = math.pi / length * (orders[None, :] + 0.5) * np.arange(length)[:, None]
    forward = np.concatenate([np.cos(angle), -np.sin(angle)], axis=1)
    return split_table(forward), split_table(forward.T / length)


def near_core(x):
    return pltpu.with_memory_space_constraint(x, pltpu.VMEM)


def call(body, out_shape, *, grid_spec=None, in_specs=None, out_specs=None, scratch=(), room=16, aliases=None, work=1):
    params = pltpu.CompilerParams(vmem_limit_bytes=room * MIB)
    cost = pl.CostEstimate(flops=work, bytes_accessed=1, transcendentals=0)
    kwargs = dict(out_shape=out_shape, compiler_params=params, cost_estimate=cost)
    if aliases:
        kwargs["input_output_aliases"] = aliases
    if grid_spec is not None:
        return pl.pallas_call(body, grid_spec=grid_spec, **kwargs)
    return pl.pallas_call(body, in_specs=in_specs, out_specs=out_specs, scratch_shapes=list(scratch), **kwargs)


def pack_body(group, slim, chunks, order, me_ref, *rest):
    sources, rest = rest[:3], rest[3:]
    outs, (gated, taps), buffers, sems = rest[:-4], rest[-4:-2], rest[-2], rest[-1]
    part = slim // chunks
    me = me_ref[0]
    low = lax.rem(me, group)
    copies = {}
    for t in order:
        start = pl.multiple_of(jnp.bitwise_xor(me // group, t) * LANES, LANES)
        for a, source in enumerate(sources):
            copies[t, a] = pltpu.make_async_copy(source.at[:, pl.ds(start, LANES)], buffers.at[a, t], sems.at[a, t])
            copies[t, a].start()
    for t in order:
        for a in range(3):
            copies[t, a].wait()
        gated[...] = (buffers[0, t] * buffers[1, t]).T
        taps[...] = buffers[2, t].T
        for e in range(group):
            start = jnp.bitwise_xor(low, e) * slim
            for k in range(chunks):
                rows = pl.ds(pl.multiple_of(start + k * part, 8), part)
                out = outs[(t * group + e) * chunks + k]
                out[0:part, :] = gated[rows, :]
                out[part : 2 * part, :] = taps[rows, :]


def pack(me, key_rows, value_rows, filters, count, chunks):
    length, channels = key_rows.shape
    slim = channels // count
    group = LANES // slim
    steps = count // group
    order = list(range(steps // 2, steps)) + list(range(steps // 2))
    hbm = pl.BlockSpec(memory_space=pltpu.HBM)
    vmem = pl.BlockSpec(memory_space=pltpu.VMEM)
    return call(
        functools.partial(pack_body, group, slim, chunks, order),
        [jax.ShapeDtypeStruct((2 * slim // chunks, length), f32)] * (count * chunks),
        in_specs=[pl.BlockSpec(memory_space=pltpu.SMEM)] + [hbm] * 3,
        out_specs=[vmem] * (count * chunks),
        scratch=[
            pltpu.VMEM((LANES, length), f32),
            pltpu.VMEM((LANES, length), f32),
            pltpu.VMEM((3, steps, length, LANES), f32),
            pltpu.SemaphoreType.DMA((3, steps)),
        ],
        room=8,
    )(me, *(pltpu.with_memory_space_constraint(x, pltpu.HBM) for x in (key_rows, value_rows, filters)))


def spectrum_body(*refs):
    arrived, (fwd_high, fwd_low), out = refs[:-3], refs[-3:-1], refs[-1]
    rows = jnp.concatenate([ref[...] for ref in arrived], axis=0)
    high, low = halves(rows)
    out[...] = dot_split(high, low, fwd_high[...], fwd_low[...])


def spectrum(arrived, forward):
    double, length = arrived[0].shape
    vmem = pl.BlockSpec(memory_space=pltpu.VMEM)
    return call(
        spectrum_body,
        jax.ShapeDtypeStruct((len(arrived) * double, 2 * length), f32),
        in_specs=[vmem] * (2 + len(arrived)),
        out_specs=vmem,
        room=16,
    )(*arrived, *forward)


def products(count, part, length, spectra, totals):
    lane_steps = length // LANES

    def tile(index, carry):
        group = index // lane_steps
        lane = lax.rem(index, lane_steps)
        sign = jnp.where(lane * 2 < lane_steps, 1.0, -1.0).astype(f32)
        top = pl.ds(pl.multiple_of(group * 8, 8), 8)
        bottom = pl.ds(pl.multiple_of(part + group * 8, 8), 8)
        re = pl.ds(pl.multiple_of(lane * LANES, LANES), LANES)
        im = pl.ds(pl.multiple_of(length + lane * LANES, LANES), LANES)
        gated_re = [spectra[p, top, re] for p in range(count)]
        gated_im = [spectra[p, top, im] for p in range(count)]
        taps_re, taps_im = [], []
        last_re = last_im = None
        for q in range(count):
            now_re, now_im = spectra[q, bottom, re], spectra[q, bottom, im]
            if q == 0:
                taps_re.append(now_re)
                taps_im.append(now_im)
            else:
                taps_re.append(now_re - sign * last_im)
                taps_im.append(now_im + sign * last_re)
            last_re, last_im = now_re, now_im
        for i in range(count):
            total_re = total_im = None
            for p in range(i + 1):
                a_re, a_im = gated_re[p], gated_im[p]
                b_re, b_im = taps_re[i - p], taps_im[i - p]
                one_re = a_re * b_re - a_im * b_im
                one_im = a_re * b_im + a_im * b_re
                total_re = one_re if p == 0 else total_re + one_re
                total_im = one_im if p == 0 else total_im + one_im
            totals[i, top, re] = total_re
            totals[i, top, im] = total_im
        return carry

    lax.fori_loop(0, part // 8 * lane_steps, tile, 0)


def conv_body(early, late, far, me_ref, fwd_high, fwd_low, inv_high, inv_low, *rest):
    arrived, rest = rest[: len(late)], rest[len(late) :]
    known, rest = rest[: len(early)], rest[len(early) :]
    outs, (left, spectra, totals) = rest[: len(far)], rest[len(far) :]
    count = sum(map(len, early)) + len(late)
    near = [s for s in range(count) if s not in far]
    me = me_ref[0]
    double, length = arrived[0].shape
    part = double // 2
    for group, one in zip(early, known):
        for e, s in enumerate(group):
            spectra[jnp.bitwise_xor(me, s)] = one[e * double : (e + 1) * double, :]
    rows = jnp.concatenate([ref[...] for ref in arrived], axis=0)
    high, low = halves(rows)
    result = dot_split(high, low, fwd_high[...], fwd_low[...])
    for e, s in enumerate(late):
        spectra[jnp.bitwise_xor(me, s)] = result[e * double : (e + 1) * double]
    products(count, part, length, spectra, totals)
    stacked = jnp.concatenate([totals[jnp.bitwise_xor(me, s)] for s in far], axis=0)
    high, low = halves(stacked)
    result = dot_split(high, low, inv_high[...], inv_low[...])
    for e in range(len(far)):
        outs[e][...] = result[e * part : (e + 1) * part]
    for e, s in enumerate(near):
        left[e * part : (e + 1) * part, :] = totals[jnp.bitwise_xor(me, s)]


def convolve(me, early, late, far, known, arrived, forward, inverse):
    count = sum(map(len, early)) + len(late)
    double, length = arrived[0].shape
    part = double // 2
    vmem = pl.BlockSpec(memory_space=pltpu.VMEM)
    return call(
        functools.partial(conv_body, early, late, far),
        [jax.ShapeDtypeStruct((part, length), f32)] * len(far)
        + [jax.ShapeDtypeStruct(((count - len(far)) * part, 2 * length), f32)],
        in_specs=[pl.BlockSpec(memory_space=pltpu.SMEM)] + [vmem] * (4 + len(late) + len(early)),
        out_specs=[vmem] * (len(far) + 1),
        scratch=[
            pltpu.VMEM((count, double, 2 * length), f32),
            pltpu.VMEM((count, part, 2 * length), f32),
        ],
        room=24,
    )(me, *forward, *inverse, *arrived, *known)


def restore_body(left, inv_high, inv_low, *outs):
    part = outs[0].shape[0]
    high, low = halves(left[...])
    result = dot_split(high, low, inv_high[...], inv_low[...])
    for e, out in enumerate(outs):
        out[...] = result[e * part : (e + 1) * part]


def restore(left, inverse, pieces):
    rows, width = left.shape
    vmem = pl.BlockSpec(memory_space=pltpu.VMEM)
    return call(
        restore_body,
        [jax.ShapeDtypeStruct((rows // pieces, width // 2), f32)] * pieces,
        in_specs=[vmem] * 3,
        out_specs=[vmem] * pieces,
        room=16,
    )(left, *inverse)


def gates_body(count, chunks, me_ref, query_ref, key_ref, value_ref, skip_ref, gate_ref, direct_ref, gate_t, direct_t):
    query = query_ref[...]
    gate_t[...] = query.T
    direct_t[...] = (query * (skip_ref[...] * (key_ref[...] * value_ref[...]))).T
    slim = gate_t.shape[0] // count
    part = slim // chunks
    for k in range(chunks):
        for s in range(count):
            start = jnp.bitwise_xor(me_ref[0], s) * slim + k * part
            source = pl.ds(pl.multiple_of(start, 8), part)
            here = pl.ds((k * count + s) * part, part)
            gate_ref[here, :] = gate_t[source, :]
            direct_ref[here, :] = direct_t[source, :]


def gates(me, query_rows, key_rows, value_rows, skip_gain, count, chunks):
    length, channels = query_rows.shape
    vmem = pl.BlockSpec(memory_space=pltpu.VMEM)
    return call(
        functools.partial(gates_body, count, chunks),
        [jax.ShapeDtypeStruct((channels, length), f32)] * 2,
        in_specs=[pl.BlockSpec(memory_space=pltpu.SMEM)] + [vmem] * 4,
        out_specs=[vmem] * 2,
        scratch=[pltpu.VMEM((channels, length), f32)] * 2,
        room=16,
        work=8 * 10**10,
    )(me, query_rows, key_rows, value_rows, skip_gain[None, :])


def mix_body(first, chained, *refs):
    out, whole = refs[-2:]
    *pieces, gate, direct = refs[: len(refs) - 2 - chained]
    part = pieces[0].shape[0]
    for e, piece in enumerate(pieces):
        rows = pl.ds((first + e) * part, part)
        mixed = gate[rows, :] * piece[...] + direct[rows, :]
        out[e * part : (e + 1) * part, :] = mixed
        whole[rows, :] = mixed


def mix(pieces, gate, direct, first, whole):
    part, length = pieces[0].shape
    count = len(pieces)
    vmem = pl.BlockSpec(memory_space=pltpu.VMEM)
    chained = [] if whole is None else [whole]
    return call(
        functools.partial(mix_body, first, len(chained)),
        [jax.ShapeDtypeStruct((count * part, length), f32), jax.ShapeDtypeStruct(gate.shape, f32)],
        in_specs=[vmem] * (count + 2 + len(chained)),
        out_specs=[vmem] * 2,
        room=8,
        aliases={count + 2: 1} if chained else None,
    )(*pieces, gate, direct, *chained)


def cut_body(weight_ref, out_ref):
    out_ref[0] = weight_ref[...]


def cut(out_weight, peers):
    channels, total = out_weight.shape
    width = total // peers
    return call(
        cut_body,
        jax.ShapeDtypeStruct((peers, channels, width), f32),
        grid_spec=pl.GridSpec(
            grid=(peers,),
            in_specs=[pl.BlockSpec((channels, width), lambda o: (0, o))],
            out_specs=pl.BlockSpec((1, channels, width), lambda o: (o, 0, 0)),
        ),
        room=8,
    )(pltpu.with_memory_space_constraint(out_weight, pltpu.HBM))


def weights_body(count, chunks, me_ref, mine_ref, weight_ref, high_ref, low_ref, ordered):
    slim = ordered.shape[0] // count
    part = slim // chunks
    for k in range(chunks):
        for s in range(count):
            start = jnp.bitwise_xor(me_ref[0], s) * slim + k * part
            ordered[pl.ds((k * count + s) * part, part), :] = weight_ref[0, pl.ds(pl.multiple_of(start, 8), part), :]
    high, low = halves(ordered[...].T)
    high_ref[...] = high
    low_ref[...] = low


def weights(me, mine, blocks, count, chunks):
    peers, channels, width = blocks.shape
    result = pl.BlockSpec((width, channels), lambda o, me_ref, mine_ref: (0, o))
    return call(
        functools.partial(weights_body, count, chunks),
        [jax.ShapeDtypeStruct((width, peers * channels), bf16)] * 2,
        grid_spec=pltpu.PrefetchScalarGridSpec(
            num_scalar_prefetch=2,
            grid=(peers,),
            in_specs=[pl.BlockSpec((1, channels, width), lambda o, me_ref, mine_ref: (jnp.bitwise_xor(mine_ref[0], o), 0, 0))],
            out_specs=[result] * 2,
            scratch_shapes=[pltpu.VMEM((channels, width), f32)],
        ),
        room=12,
        work=3 * 10**10,
    )(me, mine, blocks)


def project_body(entries, started, final, *refs):
    count = 1 + max(entry[0] for entry in entries)
    before, refs = refs[:started], refs[started:]
    mixed, (table_high, table_low), rest = refs[:count], refs[count : count + 2], refs[count + 2 :]
    rows = jnp.concatenate([mixed[i][a : a + n, :] for i, a, n, _ in entries], axis=0)
    high, low = halves(rows)
    out = rest[0]
    steps = 4 if final else 1
    span = out.shape[0] // steps
    copies = []
    for r in range(steps):
        here = pl.ds(r * span, span)
        w_high = jnp.concatenate([table_high[here, c : c + n] for _, _, n, c in entries], axis=1)
        w_low = jnp.concatenate([table_low[here, c : c + n] for _, _, n, c in entries], axis=1)
        total = dot_split(w_high, w_low, high, low)
        if started:
            total = total + before[0][here, :]
        if final:
            held, sems = rest[-2:]
            held[here, :] = total
            copies.append(pltpu.make_async_copy(held.at[here, :], out.at[here, :], sems.at[r]))
            copies[-1].start()
        else:
            out[...] = total
    for copy in copies:
        copy.wait()


def project(entries, tables, total=None, final=False, work=1):
    arrays, places = [], []
    for array, *place in entries:
        found = [i for i, other in enumerate(arrays) if other is array]
        if not found:
            arrays.append(array)
        places.append((found[0] if found else len(arrays) - 1, *place))
    length = arrays[0].shape[1]
    high, low = tables
    width = high.shape[0]
    vmem = pl.BlockSpec(memory_space=pltpu.VMEM)
    started = total is not None
    return call(
        functools.partial(project_body, places, started, final),
        jax.ShapeDtypeStruct((width, length), f32),
        in_specs=[vmem] * (len(arrays) + 2 + started),
        out_specs=pl.BlockSpec(memory_space=pltpu.HBM) if final else vmem,
        scratch=[pltpu.VMEM((width, length), f32), pltpu.SemaphoreType.DMA((4,))] if final else [],
        room=16,
        work=work,
    )(*([total] * started), *map(near_core, arrays), high, low)


def swap(x, axis, size, offset):
    return lax.ppermute(x, axis, [(j, j ^ offset) for j in range(size)])


def spread(x, bit):
    found = {0: x}
    for o in range(1, bit):
        found[o] = swap(found[o & (o - 1)], "ch", lax.axis_size("ch"), o & -o)
    return found


def after(value, others):
    return lax.optimization_barrier((value, others))[0]


def per_device(query_rows, key_rows, value_rows, filters, skip_gain, out_weight):
    count = lax.axis_size("seq")
    peers = lax.axis_size("ch")
    length, channels = query_rows.shape
    slim = channels // count
    chunks = max(1, min(CHUNKS, slim // 8))
    width = out_weight.shape[1] // peers
    me = lax.axis_index("seq").astype(jnp.int32).reshape(1)
    mine = lax.axis_index("ch").astype(jnp.int32)
    forward, inverse = transforms(length)

    pieces = pack(me, key_rows, value_rows, filters, count, chunks)
    sent = [pieces[k::chunks] for k in range(chunks)]
    half = count // 2
    near, far = list(range(half)), list(range(half, count))
    arrived = [[None] * count for _ in range(chunks)]
    for k in range(chunks):
        for s in far:
            arrived[k][s] = swap(sent[k][s], "seq", count, s)
        for s in near[1:]:
            piece = sent[k][s] if s < 3 else after(sent[k][s], arrived[k][s - 1])
            arrived[k][s] = swap(piece, "seq", count, s)
        arrived[k][0] = sent[k][0]
    blocks = cut(after(out_weight, sent[0][half]), peers)
    blocks = lax.all_to_all(blocks, "ch", split_axis=0, concat_axis=0, tiled=True)

    gate, direct = gates(me, query_rows, key_rows, value_rows, skip_gain, count, chunks)
    early, late = [near], far
    part = slim // chunks
    units = [near, far]
    if half // 2 * part % LANES == 0:
        units = [near, far[: half // 2], far[half // 2 :]]
    total = None
    tables = None
    for k in range(chunks):
        known = [spectrum([arrived[k][s] for s in group], forward) for group in early]
        last = [arrived[k][s] for s in late]
        last, known, gate, direct = lax.optimization_barrier((last, known, gate, direct))
        back = [None] * count
        *pieces, left = convolve(me, early, late, far, known, last, forward, inverse)
        for s, piece in zip(far, pieces):
            back[s] = swap(piece, "seq", count, s)
        for s, piece in zip(near, restore(left, inverse, half)):
            back[s] = swap(piece, "seq", count, s) if s else piece
        if tables is None:
            tables = weights(after(me, left), mine.reshape(1), blocks, count, chunks)
        bit = peers // 2
        own, far_own, whole = [], [], None
        last = len(units) - 1
        starts = [unit[0] * part for unit in units]
        sizes = [len(unit) * part for unit in units]

        def entry(array, u, o, row=0):
            return (array, row, sizes[u], o * channels + starts[u])

        for u, unit in enumerate(units):
            pieces = [back[s] for s in unit]
            if u:
                total = project([entry(own[u - 1], u - 1, 0)], tables, total, work=3 * 10**10)
                total, pieces = lax.optimization_barrier((total, pieces))
            alone, whole = mix(pieces, gate, direct, unit[0], whole)
            own.append(alone)
            far_own.append(swap(alone, "ch", peers, bit))

    beside = spread(whole, bit)
    across = [spread(after(x, own[last]), bit) for x in far_own[:last]]
    total = project([entry(own[last], last, 0), entry(across[0][0], 0, bit)], tables, total, work=3 * 10**10)
    total = project([(beside[o], 0, channels, o * channels) for o in range(1, bit)], tables, total, work=3 * 10**10)
    if last > 1:
        entries = [entry(across[u][0], u, bit) for u in range(1, last)]
        entries += [entry(across[u][o], u, bit | o) for u in range(last - 1) for o in range(1, bit)]
        total = project(entries, tables, total, work=3 * 10**10)
    total, ending = lax.optimization_barrier((total, far_own[last]))
    ending = spread(ending, bit)
    entries = [entry(ending[0], last, bit)]
    entries += [entry(across[last - 1][o], last - 1, bit | o) for o in range(1, bit)]
    total = project(entries, tables, total)
    total = project([entry(ending[o], last, bit | o) for o in range(1, bit)], tables, total, True)
    return total


def solution(mesh):
    in_specs = (
        P("seq", "ch"),
        P("seq", "ch"),
        P("seq", "ch"),
        P("seq", "ch"),
        P("ch"),
        P("ch", None),
    )
    out_specs = P("ch", "seq")
    return jax.shard_map(
        per_device, mesh=mesh, in_specs=in_specs, out_specs=out_specs, check_vma=False
    )
```

time: 115 us -> 103 us (0.90)
  the two profiles are of different devices: /device:TPU:9 before, /device:TPU:0 now
where the time goes in v1:
time: 103 us; the launch traced here: 102 us
  starting transfers between devices  36.7 us (36%)
  Pallas kernels  31.1 us (30%)
  waiting for transfers between devices  26.5 us (26%)
  local copies, waits for them, and re-layouts  7.46 us (7%)
    ppermute x21, starting transfers between devices, swap(): return lax.ppermute(x, axis, [(j, j ^ offset) for j in range(size)])  31.7 us
    ppermute x21, waiting for transfers between devices, swap(): return lax.ppermute(x, axis, [(j, j ^ offset) for j in range(size)])  26.5 us
    pallas_call x7, Pallas kernels, project(): call(functools.partial(project_body, places, started, final), jax.ShapeDt...  8.15 us
    unnamed x30, local copies, waits for them, and re-layouts  7.46 us
    pallas_call x1, Pallas kernels, convolve(): call(functools.partial(conv_body, early, late, far), [jax.ShapeDtypeStruc...  6.7 us
    all_to_all x1, starting transfers between devices, per_device(): lax.all_to_all(blocks, 'ch', split_axis=0, concat_axis=0, tiled=True)  5 us
    pallas_call x1, Pallas kernels, weights(): call(functools.partial(weights_body, count, chunks), [jax.ShapeDtypeStruc...  3.83 us
    pallas_call x1, Pallas kernels, pack(): call(functools.partial(pack_body, group, slim, chunks, order), [jax.Shape...  3.02 us
  transfers between devices with their start and end apart: 22, of which 5 were waited for; matrix products, arithmetic and copies ran while one was open for 0% of the time, Pallas kernels for 26%

profile of v1, /device:TPU:0, one launch (start us, length us, event | category | flops | bytes accessed | tf_op | source)
XLA Modules:
  0.0 102.0 jit_solution(18346983951780781673)
XLA Ops:
  0.0 3.0 %shard_map.100 = (f32[128,512]{1,0:T(8,128)S(1)}, f32[128,512]{1,0:T(8,128)S(1)}, f32[128,512]{1,0:T(8,128)S(1)}, f32[128,512]{1,0:T(8,128)}, f32[128,512]{1,0:T...) custom-call(s32[1]{0:T(128)} %bitcast.me_ref, f32[512,512]{1,0:T(8,128)} %key_ref.1, ...), custom_call_target="tpu_custom_call" | custom-call | flops 1 | bytes 1 | tf_op jit(solution)/shard_map/pallas_call | solution.py:96
  3.0 3.1 %collective-permute-start.5 = (f32[128,512]{1,0:T(8,128)S(1)}, f32[128,512]{1,0:T(8,128)S(1)}, u32[]{:S(2)}, u32[]{:S(2)}) collective-permute-start(f32[128,512]{1,0:T(8,128)S(1)} %get-tuple-element.58), channel_id=1, source_target_pairs={{0,8},{4,12},{8,0},{12,4},{16,24},{20,28},{24,16},{28,20},{1,9},{5... | collective-permute-start | bytes 786440 | tf_op jit(solution)/shard_map/ppermute | solution.py:392
  6.1 1.5 %collective-permute-start.4 = (f32[128,512]{1,0:T(8,128)S(1)}, f32[128,512]{1,0:T(8,128)S(1)}, u32[]{:S(2)}, u32[]{:S(2)}) collective-permute-start(f32[128,512]{1,0:T(8,128)S(1)} %get-tuple-element.57), channel_id=1, source_target_pairs={{0,4},{4,0},{8,12},{12,8},{16,20},{20,16},{24,28},{28,24},{1,5},{5... | collective-permute-start | bytes 786440 | tf_op jit(solution)/shard_map/ppermute | solution.py:392
  7.6 2.6 %collective-permute-start = (f32[128,512]{1,0:T(8,128)}, f32[128,512]{1,0:T(8,128)}, u32[]{:S(2)}, u32[]{:S(2)}) collective-permute-start(f32[128,512]{1,0:T(8,128)} %get-tuple-element.52), channel_id=1, source_target_pairs={{0,16},{4,20},{8,24},{12,28},{16,0},{20,4},{24,8},{28,12},{1,17},{... | collective-permute-start | bytes 786440 | tf_op jit(solution)/shard_map/ppermute | solution.py:392
  10.2 0.3 collective-permute-start.1
  10.5 2.5 %collective-permute-start.2 = (f32[128,512]{1,0:T(8,128)}, f32[128,512]{1,0:T(8,128)}, u32[]{:S(2)}, u32[]{:S(2)}) collective-permute-start(f32[128,512]{1,0:T(8,128)} %get-tuple-element.54), channel_id=1, source_target_pairs={{0,24},{4,28},{8,16},{12,20},{16,8},{20,12},{24,0},{28,4},{1,25},{... | collective-permute-start | bytes 786440 | tf_op jit(solution)/shard_map/ppermute | solution.py:392
  13.0 3.0 %shard_map.106 = f32[4,512,512]{2,1,0:T(8,128)S(1)} custom-call(f32[512,2048]{1,0:T(8,128)} %weight_ref), custom_call_target="tpu_custom_call" | custom-call | flops 1 | bytes 1 | tf_op jit(solution)/shard_map/pallas_call | solution.py:298
  16.0 2.0 %copy-done = f32[4,512,512]{2,1,0:T(8,128)} copy-done((f32[4,512,512]{2,1,0:T(8,128)}, f32[4,512,512]{2,1,0:T(8,128)S(1)}, u32[]{:S(2)}) %copy-start) | copy-done | bytes 4194328
  18.0 5.0 %all-to-all-start = ((f32[4,512,512]{2,1,0:T(8,128)}), f32[4,512,512]{2,1,0:T(8,128)}, u32[]{:S(2)}, u32[]{:S(2)}) async-start(f32[4,512,512]{2,1,0:T(8,128)} %copy-done), calls=%async_computation | async-start | bytes 8388608 | tf_op jit(solution)/shard_map/all_to_all | solution.py:430
  23.0 0.7 copy-done.7
  23.7 2.3 %collective-permute-start.3 = (f32[128,512]{1,0:T(8,128)}, f32[128,512]{1,0:T(8,128)S(1)}, u32[]{:S(2)}, u32[]{:S(2)}) collective-permute-start(f32[128,512]{1,0:T(8,128)} %get-tuple-element.55), channel_id=1, source_target_pairs={{0,28},{4,24},{8,20},{12,16},{16,12},{20,8},{24,4},{28,0},{1,29},{... | collective-permute-start | bytes 786440 | tf_op jit(solution)/shard_map/ppermute | solution.py:392
  26.0 0.7 copy-done.9
  26.8 1.2 %copy-done.6 = f32[512,512]{1,0:T(8,128)S(1)} copy-done((f32[512,512]{1,0:T(8,128)S(1)}, f32[512,512]{1,0:T(8,128)}, u32[]{:S(2)}) %copy-start.6) | copy-done | bytes 1048600
  28.0 1.2 %copy-done.13 = f32[512,512]{1,0:T(8,128)S(1)} copy-done((f32[512,512]{1,0:T(8,128)S(1)}, f32[512,512]{1,0:T(8,128)}, u32[]{:S(2)}) %copy-start.13) | copy-done | bytes 1048600
  29.2 0.7 shard_map.102
  29.9 0.0 copy-start.1
  29.9 0.0 copy-start.2
  30.0 20.0 %collective-permute-done.6.refs_3_ = f32[128,512]{1,0:T(8,128)S(1)} collective-permute-done((f32[128,512]{1,0:T(8,128)}, f32[128,512]{1,0:T(8,128)S(1)}, u32[]{:S(2)}, u32[]{:S(2)}) %collective-permute-start.6) | collective-permute-done | bytes 262176 | tf_op jit(solution)/shard_map/ppermute | solution.py:392
  49.9 1.8 %shard_map.101.rest_4_ = f32[512,1024]{1,0:T(8,128)S(1)} custom-call(f32[128,512]{1,0:T(8,128)S(1)} %get-tuple-element.56.refs_0_, f32[128,512]{1,0:T(8,128)S(1)} %copy-done.10, f32[128,512]{1,0:T(8,128)S(1)} %copy-done.8, f32[128,512]{1,0:T(8,128)S(1)} %collective-permute-done.6.refs_3_, bf16[512,1024]{1,0:T(8,128)(2,1)S(1)} %copy-done.3, ...), custom_call_target="tpu_custom_call" | custom-call | flops 1 | bytes 1 | tf_op jit(solution)/shard_map/pallas_call | solution.py:121
  51.8 6.7 %shard_map.103 = (f32[64,512]{1,0:T(8,128)}, f32[64,512]{1,0:T(8,128)}, f32[64,512]{1,0:T(8,128)}, f32[64,512]{1,0:T(8,128)}, f32[256,1024]{1,0:T(8,128)S(1)}) custom-call(s32[1]{0:T(128)} %bitcast.me_ref, bf16[512,1024]{1,0:T(8,128)(2,1)S(1)} %copy-done.3, bf16[512,1024]{1,0:T(8,128)(2,1)S(1)} %copy-done.4, bf16[1024,512]{1,0:T(8,128)(2,1)S(1)} %copy-done.1, ...), custom_call_target="tpu_custom_call" | custom-call | flops 1 | bytes 1 | tf_op jit(solution)/shard_map/pallas_call | solution.py:202
  58.5 1.0 shard_map.104
  59.5 1.6 %collective-permute-start.7 = (f32[64,512]{1,0:T(8,128)S(1)}, f32[64,512]{1,0:T(8,128)S(1)}, u32[]{:S(2)}, u32[]{:S(2)}) collective-permute-start(f32[64,512]{1,0:T(8,128)S(1)} %get-tuple-element.70), channel_id=1, source_target_pairs={{0,4},{4,0},{8,12},{12,8},{16,20},{20,16},{24,28},{28,24},{1,5},{5... | collective-permute-start | bytes 393224 | tf_op jit(solution)/shard_map/ppermute | solution.py:392
  61.0 4.3 %collective-permute-start.8 = (f32[64,512]{1,0:T(8,128)S(1)}, f32[64,512]{1,0:T(8,128)S(1)}, u32[]{:S(2)}, u32[]{:S(2)}) collective-permute-start(f32[64,512]{1,0:T(8,128)S(1)} %get-tuple-element.71), channel_id=1, source_target_pairs={{0,8},{4,12},{8,0},{12,4},{16,24},{20,28},{24,16},{28,20},{1,9},{5... | collective-permute-start | bytes 393224 | tf_op jit(solution)/shard_map/ppermute | solution.py:392
  65.4 3.0 %collective-permute-start.10 = (f32[64,512]{1,0:T(8,128)}, f32[64,512]{1,0:T(8,128)}, u32[]{:S(2)}, u32[]{:S(2)}) collective-permute-start(f32[64,512]{1,0:T(8,128)} %get-tuple-element.80), channel_id=1, source_target_pairs={{0,16},{4,20},{8,24},{12,28},{16,0},{20,4},{24,8},{28,12},{1,17},{... | collective-permute-start | bytes 393224 | tf_op jit(solution)/shard_map/ppermute | solution.py:392
  68.4 0.9 collective-permute-start.11
  69.3 2.4 %collective-permute-start.12 = (f32[64,512]{1,0:T(8,128)}, f32[64,512]{1,0:T(8,128)}, u32[]{:S(2)}, u32[]{:S(2)}) collective-permute-start(f32[64,512]{1,0:T(8,128)} %get-tuple-element.87), channel_id=1, source_target_pairs={{0,24},{4,28},{8,16},{12,20},{16,8},{20,12},{24,0},{28,4},{1,25},{... | collective-permute-start | bytes 393224 | tf_op jit(solution)/shard_map/ppermute | solution.py:392
  71.7 3.1 %collective-permute-start.13 = (f32[64,512]{1,0:T(8,128)}, f32[64,512]{1,0:T(8,128)}, u32[]{:S(2)}, u32[]{:S(2)}) collective-permute-start(f32[64,512]{1,0:T(8,128)} %get-tuple-element.88), channel_id=1, source_target_pairs={{0,28},{4,24},{8,20},{12,16},{16,12},{20,8},{24,4},{28,0},{1,29},{... | collective-permute-start | bytes 393224 | tf_op jit(solution)/shard_map/ppermute | solution.py:392
  74.8 0.7 copy-done.11
  75.4 0.9 copy-done.12
  76.3 0.9 shard_map.105
  77.2 1.5 %collective-permute-start.14 = (f32[256,512]{1,0:T(8,128)}, f32[256,512]{1,0:T(8,128)}, u32[]{:S(2)}, u32[]{:S(2)}) collective-permute-start(f32[256,512]{1,0:T(8,128)} %get-tuple-element.75.refs_0_), channel_id=1, source_target_pairs={{0,2},{1,3},{2,0},{3,1},{4,6},{5,7},{6,4},{7,5},{8,10},{9,11},{10,... | collective-permute-start | bytes 1572872 | tf_op jit(solution)/shard_map/ppermute | solution.py:392
  78.7 3.8 %shard_map.107 = (bf16[512,2048]{1,0:T(8,128)(2,1)S(1)}, bf16[512,2048]{1,0:T(8,128)(2,1)S(1)}) custom-call(s32[1]{0:T(128)} %bitcast.me_ref, s32[1]{0:T(128)} %bitcast.2.mine_ref, f32[4,512,512]{2,1,0:T(8,128)} %all-to-all-done.weight_ref), custom_call_target="tpu_custom_call" | custom-call | flops 30000001024 | bytes 1 | tf_op jit(solution)/shard_map/pallas_call | solution.py:325
  82.6 1.6 %shard_map.108.refs_0_ = f32[512,512]{1,0:T(8,128)S(1)} custom-call(f32[256,512]{1,0:T(8,128)} %get-tuple-element.75.refs_0_, bf16[512,2048]{1,0:T(8,128)(2,1)S(1)} %get-tuple-element.78.refs_1_.refs_2_.refs_3_, bf16[512,2048]{1,0:T(8,128)(2,1)S(1)} %get-tuple-element.79.refs_2_.refs_3_.refs_4_), custom_call_target="tpu_custom_call" | custom-call | flops 30000001024 | bytes 1 | tf_op jit(solution)/shard_map/pallas_call | solution.py:380
  84.2 2.9 %collective-permute-done.11.refs_1_ = f32[64,512]{1,0:T(8,128)} collective-permute-done((f32[64,512]{1,0:T(8,128)}, f32[64,512]{1,0:T(8,128)}, u32[]{:S(2)}, u32[]{:S(2)}) %collective-permute-start.11) | collective-permute-done | bytes 131104 | tf_op jit(solution)/shard_map/ppermute | solution.py:392
  87.1 1.0 shard_map.109
  88.1 1.6 %collective-permute-start.16 = (f32[128,512]{1,0:T(8,128)S(1)}, f32[128,512]{1,0:T(8,128)S(1)}, u32[]{:S(2)}, u32[]{:S(2)}) collective-permute-start(f32[128,512]{1,0:T(8,128)S(1)} %get-tuple-element.86.refs_1_), channel_id=1, source_target_pairs={{0,2},{1,3},{2,0},{3,1},{4,6},{5,7},{6,4},{7,5},{8,10},{9,11},{10,... | collective-permute-start | bytes 786440 | tf_op jit(solution)/shard_map/ppermute | solution.py:392
  89.7 0.6 shard_map.110.refs_0_
  90.3 1.0 shard_map.111
  91.3 0.6 collective-permute-start.18
  91.9 0.5 collective-permute-start.17
  92.4 2.0 %shard_map.112.refs_0_ = f32[512,512]{1,0:T(8,128)S(1)} custom-call(f32[512,512]{1,0:T(8,128)S(1)} %shard_map.110.refs_0_, f32[128,512]{1,0:T(8,128)S(1)} %get-tuple-element.93.refs_1_, f32[256,512]{1,0:T(8,128)} %collective-permute-done.14.refs_2_, bf16[512,2048]{1,0:T(8,128)(2,1)S(1)} %get-tuple-element.78.refs_1_.refs_2_.refs_3_, ...), custom_call_target="tpu_custom_call" | custom-call | flops 30000001024 | bytes 1 | tf_op jit(solution)/shard_map/pallas_call | solution.py:380
  94.5 1.9 %collective-permute-done.16.refs_1_ = f32[128,512]{1,0:T(8,128)S(1)} collective-permute-done((f32[128,512]{1,0:T(8,128)S(1)}, f32[128,512]{1,0:T(8,128)S(1)}, u32[]{:S(2)}, u32[]{:S(2)}) %collective-permute-start.16) | collective-permute-done | bytes 262176 | tf_op jit(solution)/shard_map/ppermute | solution.py:392
  96.4 1.0 shard_map.113.refs_0_
  97.4 1.0 shard_map.114.refs_0_
  98.4 0.8 collective-permute-done.18.refs_1_
  99.2 0.6 shard_map.115.refs_0_
  99.8 0.9 collective-permute-done.20.refs_1_
  100.7 1.3 %shard_map.116 = f32[512,512]{1,0:T(8,128)} custom-call(f32[512,512]{1,0:T(8,128)S(1)} %shard_map.115.refs_0_, f32[128,512]{1,0:T(8,128)S(1)} %collective-permute-done.20.refs_1_, bf16[512,2048]{1,0:T(8,128)(2,1)S(1)} %get-tuple-element.78.refs_1_.refs_2_.refs_3_, bf16[512,2048]{1,0:T(8,128)(2,1)S(1)} %get-tuple-element.79.refs_2_.refs_3_.refs_4_), custom_call_target="tpu_custom_call" | custom-call | flops 1 | bytes 1 | tf_op jit(solution)/shard_map/pallas_call | solution.py:380
  (43 shorter events, 0.1 us)
Async XLA Ops:
  3.0 20.0 %collective-permute-start.5 = (f32[128,512]{1,0:T(8,128)S(1)}, f32[128,512]{1,0:T(8,128)S(1)}, u32[]{:S(2)}, u32[]{:S(2)}) collective-permute-start(f32[128,512]{1,0:T(8,128)S(1)} %get-tuple-element.58), channel_id=1, source_target_pairs={{0,8},{4,12},{8,0},{12,4},{16,24},{20,28},{24,16},{28,20},{1,9},{5... | collective-permute-start | bytes 786440 | tf_op jit(solution)/shard_map/ppermute | solution.py:392
  6.1 19.9 %collective-permute-start.4 = (f32[128,512]{1,0:T(8,128)S(1)}, f32[128,512]{1,0:T(8,128)S(1)}, u32[]{:S(2)}, u32[]{:S(2)}) collective-permute-start(f32[128,512]{1,0:T(8,128)S(1)} %get-tuple-element.57), channel_id=1, source_target_pairs={{0,4},{4,0},{8,12},{12,8},{16,20},{20,16},{24,28},{28,24},{1,5},{5... | collective-permute-start | bytes 786440 | tf_op jit(solution)/shard_map/ppermute | solution.py:392
  7.6 44.1 %collective-permute-start = (f32[128,512]{1,0:T(8,128)}, f32[128,512]{1,0:T(8,128)}, u32[]{:S(2)}, u32[]{:S(2)}) collective-permute-start(f32[128,512]{1,0:T(8,128)} %get-tuple-element.52), channel_id=1, source_target_pairs={{0,16},{4,20},{8,24},{12,28},{16,0},{20,4},{24,8},{28,12},{1,17},{... | collective-permute-start | bytes 786440 | tf_op jit(solution)/shard_map/ppermute | solution.py:392
  10.2 41.6 %collective-permute-start.1 = (f32[128,512]{1,0:T(8,128)}, f32[128,512]{1,0:T(8,128)}, u32[]{:S(2)}, u32[]{:S(2)}) collective-permute-start(f32[128,512]{1,0:T(8,128)} %get-tuple-element.53), channel_id=1, source_target_pairs={{0,20},{4,16},{8,28},{12,24},{16,4},{20,0},{24,12},{28,8},{1,21},{... | collective-permute-start | bytes 786440 | tf_op jit(solution)/shard_map/ppermute | solution.py:392
  10.5 41.3 %collective-permute-start.2 = (f32[128,512]{1,0:T(8,128)}, f32[128,512]{1,0:T(8,128)}, u32[]{:S(2)}, u32[]{:S(2)}) collective-permute-start(f32[128,512]{1,0:T(8,128)} %get-tuple-element.54), channel_id=1, source_target_pairs={{0,24},{4,28},{8,16},{12,20},{16,8},{20,12},{24,0},{28,4},{1,25},{... | collective-permute-start | bytes 786440 | tf_op jit(solution)/shard_map/ppermute | solution.py:392
  16.0 2.0 %copy-start = (f32[4,512,512]{2,1,0:T(8,128)}, f32[4,512,512]{2,1,0:T(8,128)S(1)}, u32[]{:S(2)}) copy-start(f32[4,512,512]{2,1,0:T(8,128)S(1)} %shard_map.106) | copy-start | bytes 12582916
  18.0 8.7 %copy-start.5 = (f32[512,512]{1,0:T(8,128)S(1)}, f32[512,512]{1,0:T(8,128)}, u32[]{:S(2)}) copy-start(f32[512,512]{1,0:T(8,128)} %key_ref.1) | copy-start | bytes 3145732
  18.0 8.7 %copy-start.14 = (f32[512]{0:T(512)S(1)}, f32[512]{0:T(512)}, u32[]{:S(2)}) copy-start(f32[512]{0:T(512)} %param.14) | copy-start | bytes 6148
  18.0 60.7 %all-to-all-start = ((f32[4,512,512]{2,1,0:T(8,128)}), f32[4,512,512]{2,1,0:T(8,128)}, u32[]{:S(2)}, u32[]{:S(2)}) async-start(f32[4,512,512]{2,1,0:T(8,128)} %copy-done), calls=%async_computation | async-start | bytes 8388608 | tf_op jit(solution)/shard_map/all_to_all | solution.py:430
  23.0 0.7 copy-start.7
  23.7 28.1 %collective-permute-start.3 = (f32[128,512]{1,0:T(8,128)}, f32[128,512]{1,0:T(8,128)S(1)}, u32[]{:S(2)}, u32[]{:S(2)}) collective-permute-start(f32[128,512]{1,0:T(8,128)} %get-tuple-element.55), channel_id=1, source_target_pairs={{0,28},{4,24},{8,20},{12,16},{16,12},{20,8},{24,4},{28,0},{1,29},{... | collective-permute-start | bytes 786440 | tf_op jit(solution)/shard_map/ppermute | solution.py:392
  26.0 0.7 copy-start.9
  26.7 23.2 %collective-permute-start.6 = (f32[128,512]{1,0:T(8,128)}, f32[128,512]{1,0:T(8,128)S(1)}, u32[]{:S(2)}, u32[]{:S(2)}) collective-permute-start(f32[128,512]{1,0:T(8,128)} %get-tuple-element.60), channel_id=1, source_target_pairs={{0,12},{4,8},{8,4},{12,0},{16,28},{20,24},{24,20},{28,16},{1,13},{... | collective-permute-start | bytes 786440 | tf_op jit(solution)/shard_map/ppermute | solution.py:392
  26.7 1.2 %copy-start.6 = (f32[512,512]{1,0:T(8,128)S(1)}, f32[512,512]{1,0:T(8,128)}, u32[]{:S(2)}) copy-start(f32[512,512]{1,0:T(8,128)} %value_ref.1) | copy-start | bytes 3145732
  28.0 1.2 %copy-start.13 = (f32[512,512]{1,0:T(8,128)S(1)}, f32[512,512]{1,0:T(8,128)}, u32[]{:S(2)}) copy-start(f32[512,512]{1,0:T(8,128)} %query_ref.1) | copy-start | bytes 3145732
  29.2 20.7 %copy-start.3 = (bf16[512,1024]{1,0:T(8,128)(2,1)S(1)}, bf16[512,1024]{1,0:T(8,128)(2,1)}, u32[]{:S(2)}) copy-start(bf16[512,1024]{1,0:T(8,128)(2,1)} %constant.17.clone.refs_4_.fwd_high) | copy-start | bytes 3145732
  29.2 20.7 %copy-start.4 = (bf16[512,1024]{1,0:T(8,128)(2,1)S(1)}, bf16[512,1024]{1,0:T(8,128)(2,1)}, u32[]{:S(2)}) copy-start(bf16[512,1024]{1,0:T(8,128)(2,1)} %constant.18.clone.refs_5_.fwd_low) | copy-start | bytes 3145732
  29.2 20.7 %copy-start.8 = (f32[128,512]{1,0:T(8,128)S(1)}, f32[128,512]{1,0:T(8,128)}, u32[]{:S(2)}) copy-start(f32[128,512]{1,0:T(8,128)} %copy-done.7) | copy-start | bytes 786436
  29.2 20.7 %copy-start.10 = (f32[128,512]{1,0:T(8,128)S(1)}, f32[128,512]{1,0:T(8,128)}, u32[]{:S(2)}) copy-start(f32[128,512]{1,0:T(8,128)} %copy-done.9) | copy-start | bytes 786436
  29.9 21.9 %copy-start.1 = (bf16[1024,512]{1,0:T(8,128)(2,1)S(1)}, bf16[1024,512]{1,0:T(8,128)(2,1)}, u32[]{:S(2)}) copy-start(bf16[1024,512]{1,0:T(8,128)(2,1)} %constant.19.clone.inv_high) | copy-start | bytes 3145732
  29.9 21.9 %copy-start.2 = (bf16[1024,512]{1,0:T(8,128)(2,1)S(1)}, bf16[1024,512]{1,0:T(8,128)(2,1)}, u32[]{:S(2)}) copy-start(bf16[1024,512]{1,0:T(8,128)(2,1)} %constant.20.clone.inv_low) | copy-start | bytes 3145732
  59.5 9.8 %collective-permute-start.7 = (f32[64,512]{1,0:T(8,128)S(1)}, f32[64,512]{1,0:T(8,128)S(1)}, u32[]{:S(2)}, u32[]{:S(2)}) collective-permute-start(f32[64,512]{1,0:T(8,128)S(1)} %get-tuple-element.70), channel_id=1, source_target_pairs={{0,4},{4,0},{8,12},{12,8},{16,20},{20,16},{24,28},{28,24},{1,5},{5... | collective-permute-start | bytes 393224 | tf_op jit(solution)/shard_map/ppermute | solution.py:392
  61.0 10.7 %collective-permute-start.8 = (f32[64,512]{1,0:T(8,128)S(1)}, f32[64,512]{1,0:T(8,128)S(1)}, u32[]{:S(2)}, u32[]{:S(2)}) collective-permute-start(f32[64,512]{1,0:T(8,128)S(1)} %get-tuple-element.71), channel_id=1, source_target_pairs={{0,8},{4,12},{8,0},{12,4},{16,24},{20,28},{24,16},{28,20},{1,9},{5... | collective-permute-start | bytes 393224 | tf_op jit(solution)/shard_map/ppermute | solution.py:392
  65.4 9.4 %collective-permute-start.9 = (f32[64,512]{1,0:T(8,128)S(1)}, f32[64,512]{1,0:T(8,128)S(1)}, u32[]{:S(2)}, u32[]{:S(2)}) collective-permute-start(f32[64,512]{1,0:T(8,128)S(1)} %get-tuple-element.72), channel_id=1, source_target_pairs={{0,12},{4,8},{8,4},{12,0},{16,28},{20,24},{24,20},{28,16},{1,13},{... | collective-permute-start | bytes 393224 | tf_op jit(solution)/shard_map/ppermute | solution.py:392
  65.4 18.8 %collective-permute-start.10 = (f32[64,512]{1,0:T(8,128)}, f32[64,512]{1,0:T(8,128)}, u32[]{:S(2)}, u32[]{:S(2)}) collective-permute-start(f32[64,512]{1,0:T(8,128)} %get-tuple-element.80), channel_id=1, source_target_pairs={{0,16},{4,20},{8,24},{12,28},{16,0},{20,4},{24,8},{28,12},{1,17},{... | collective-permute-start | bytes 393224 | tf_op jit(solution)/shard_map/ppermute | solution.py:392
  68.4 18.7 %collective-permute-start.11 = (f32[64,512]{1,0:T(8,128)}, f32[64,512]{1,0:T(8,128)}, u32[]{:S(2)}, u32[]{:S(2)}) collective-permute-start(f32[64,512]{1,0:T(8,128)} %get-tuple-element.81), channel_id=1, source_target_pairs={{0,20},{4,16},{8,28},{12,24},{16,4},{20,0},{24,12},{28,8},{1,21},{... | collective-permute-start | bytes 393224 | tf_op jit(solution)/shard_map/ppermute | solution.py:392
  69.3 21.0 %collective-permute-start.12 = (f32[64,512]{1,0:T(8,128)}, f32[64,512]{1,0:T(8,128)}, u32[]{:S(2)}, u32[]{:S(2)}) collective-permute-start(f32[64,512]{1,0:T(8,128)} %get-tuple-element.87), channel_id=1, source_target_pairs={{0,24},{4,28},{8,16},{12,20},{16,8},{20,12},{24,0},{28,4},{1,25},{... | collective-permute-start | bytes 393224 | tf_op jit(solution)/shard_map/ppermute | solution.py:392
  71.7 18.6 %collective-permute-start.13 = (f32[64,512]{1,0:T(8,128)}, f32[64,512]{1,0:T(8,128)}, u32[]{:S(2)}, u32[]{:S(2)}) collective-permute-start(f32[64,512]{1,0:T(8,128)} %get-tuple-element.88), channel_id=1, source_target_pairs={{0,28},{4,24},{8,20},{12,16},{16,12},{20,8},{24,4},{28,0},{1,29},{... | collective-permute-start | bytes 393224 | tf_op jit(solution)/shard_map/ppermute | solution.py:392
  74.8 0.7 copy-start.11
  75.4 0.9 copy-start.12
  77.2 14.7 %collective-permute-start.14 = (f32[256,512]{1,0:T(8,128)}, f32[256,512]{1,0:T(8,128)}, u32[]{:S(2)}, u32[]{:S(2)}) collective-permute-start(f32[256,512]{1,0:T(8,128)} %get-tuple-element.75.refs_0_), channel_id=1, source_target_pairs={{0,2},{1,3},{2,0},{3,1},{4,6},{5,7},{6,4},{7,5},{8,10},{9,11},{10,... | collective-permute-start | bytes 1572872 | tf_op jit(solution)/shard_map/ppermute | solution.py:392
  88.1 8.2 %collective-permute-start.16 = (f32[128,512]{1,0:T(8,128)S(1)}, f32[128,512]{1,0:T(8,128)S(1)}, u32[]{:S(2)}, u32[]{:S(2)}) collective-permute-start(f32[128,512]{1,0:T(8,128)S(1)} %get-tuple-element.86.refs_1_), channel_id=1, source_target_pairs={{0,2},{1,3},{2,0},{3,1},{4,6},{5,7},{6,4},{7,5},{8,10},{9,11},{10,... | collective-permute-start | bytes 786440 | tf_op jit(solution)/shard_map/ppermute | solution.py:392
  91.3 7.8 %collective-permute-start.18 = (f32[128,512]{1,0:T(8,128)S(1)}, f32[128,512]{1,0:T(8,128)S(1)}, u32[]{:S(2)}, u32[]{:S(2)}) collective-permute-start(f32[128,512]{1,0:T(8,128)S(1)} %get-tuple-element.93.refs_1_), channel_id=1, source_target_pairs={{0,2},{1,3},{2,0},{3,1},{4,6},{5,7},{6,4},{7,5},{8,10},{9,11},{10,... | collective-permute-start | bytes 786440 | tf_op jit(solution)/shard_map/ppermute | solution.py:392
  91.9 4.5 %collective-permute-start.15 = (f32[512,512]{1,0:T(8,128)S(1)}, f32[512,512]{1,0:T(8,128)S(1)}, u32[]{:S(2)}, u32[]{:S(2)}) collective-permute-start(f32[512,512]{1,0:T(8,128)S(1)} %get-tuple-element.95), channel_id=1, source_target_pairs={{0,1},{1,0},{2,3},{3,2},{4,5},{5,4},{6,7},{7,6},{8,9},{9,8},{10,11... | collective-permute-start | bytes 3145736 | tf_op jit(solution)/shard_map/ppermute | solution.py:392
  91.9 5.5 %collective-permute-start.17 = (f32[256,512]{1,0:T(8,128)}, f32[256,512]{1,0:T(8,128)S(1)}, u32[]{:S(2)}, u32[]{:S(2)}) collective-permute-start(f32[256,512]{1,0:T(8,128)} %collective-permute-done.14.refs_2_), channel_id=1, source_target_pairs={{0,1},{1,0},{2,3},{3,2},{4,5},{5,4},{6,7},{7,6},{8,9},{9,8},{10,11... | collective-permute-start | bytes 1572872 | tf_op jit(solution)/shard_map/ppermute | solution.py:392
  96.4 2.8 %collective-permute-start.19 = (f32[128,512]{1,0:T(8,128)S(1)}, f32[128,512]{1,0:T(8,128)S(1)}, u32[]{:S(2)}, u32[]{:S(2)}) collective-permute-start(f32[128,512]{1,0:T(8,128)S(1)} %collective-permute-done.16.refs_1_), channel_id=1, source_target_pairs={{0,1},{1,0},{2,3},{3,2},{4,5},{5,4},{6,7},{7,6},{8,9},{9,8},{10,11... | collective-permute-start | bytes 786440 | tf_op jit(solution)/shard_map/ppermute | solution.py:392
  99.2 1.5 %collective-permute-start.20 = (f32[128,512]{1,0:T(8,128)S(1)}, f32[128,512]{1,0:T(8,128)S(1)}, u32[]{:S(2)}, u32[]{:S(2)}) collective-permute-start(f32[128,512]{1,0:T(8,128)S(1)} %collective-permute-done.18.refs_1_), channel_id=1, source_target_pairs={{0,1},{1,0},{2,3},{3,2},{4,5},{5,4},{6,7},{7,6},{8,9},{9,8},{10,11... | collective-permute-start | bytes 786440 | tf_op jit(solution)/shard_map/ppermute | solution.py:392

commit v2 on v1

--- a/solution.py
+++ b/solution.py
@@ -108,23 +108,28 @@
     )(me, *(pltpu.with_memory_space_constraint(x, pltpu.HBM) for x in (key_rows, value_rows, filters)))
 
 
-def spectrum_body(*refs):
-    arrived, (fwd_high, fwd_low), out = refs[:-3], refs[-3:-1], refs[-1]
+def spectrum_body(slots, chained, me_ref, fwd_high, fwd_low, *refs):
+    arrived, out = refs[: len(slots)], refs[-1]
+    double = arrived[0].shape[0]
     rows = jnp.concatenate([ref[...] for ref in arrived], axis=0)
     high, low = halves(rows)
-    out[...] = dot_split(high, low, fwd_high[...], fwd_low[...])
-
-
-def spectrum(arrived, forward):
+    result = dot_split(high, low, fwd_high[...], fwd_low[...])
+    for e, s in enumerate(slots):
+        out[jnp.bitwise_xor(me_ref[0], s)] = result[e * double : (e + 1) * double]
+
+
+def spectrum(me, slots, arrived, forward, count, spectra):
     double, length = arrived[0].shape
     vmem = pl.BlockSpec(memory_space=pltpu.VMEM)
-    return call(
-        spectrum_body,
-        jax.ShapeDtypeStruct((len(arrived) * double, 2 * length), f32),
-        in_specs=[vmem] * (2 + len(arrived)),
+    chained = [] if spectra is None else [spectra]
+    return call(
+        functools.partial(spectrum_body, slots, len(chained)),
+        jax.ShapeDtypeStruct((count, double, 2 * length), f32),
+        in_specs=[pl.BlockSpec(memory_space=pltpu.SMEM)] + [vmem] * (2 + len(arrived) + len(chained)),
         out_specs=vmem,
         room=16,
-    )(*arrived, *forward)
+        aliases={3 + len(arrived): 0} if chained else None,
+    )(me, *forward, *arrived, *chained)
 
 
 def products(count, part, length, spectra, totals):
@@ -151,34 +156,27 @@
                 taps_re.append(now_re - sign * last_im)
                 taps_im.append(now_im + sign * last_re)
             last_re, last_im = now_re, now_im
+        gated_sum = [a + b for a, b in zip(gated_re, gated_im)]
+        taps_sum = [a + b for a, b in zip(taps_re, taps_im)]
         for i in range(count):
-            total_re = total_im = None
-            for p in range(i + 1):
-                a_re, a_im = gated_re[p], gated_im[p]
-                b_re, b_im = taps_re[i - p], taps_im[i - p]
-                one_re = a_re * b_re - a_im * b_im
-                one_im = a_re * b_im + a_im * b_re
-                total_re = one_re if p == 0 else total_re + one_re
-                total_im = one_im if p == 0 else total_im + one_im
-            totals[i, top, re] = total_re
-            totals[i, top, im] = total_im
+            reals, imags, sums = (
+                sum(a[p] * b[i - p] for p in range(1, i + 1)) + a[0] * b[i]
+                for a, b in ((gated_re, taps_re), (gated_im, taps_im), (gated_sum, taps_sum))
+            )
+            totals[i, top, re] = reals - imags
+            totals[i, top, im] = sums - reals - imags
         return carry
 
     lax.fori_loop(0, part // 8 * lane_steps, tile, 0)
 
 
-def conv_body(early, late, far, me_ref, fwd_high, fwd_low, inv_high, inv_low, *rest):
-    arrived, rest = rest[: len(late)], rest[len(late) :]
-    known, rest = rest[: len(early)], rest[len(early) :]
+def conv_body(late, far, count, me_ref, fwd_high, fwd_low, inv_high, inv_low, *rest):
+    arrived, rest = rest[: len(late)], rest[len(late) + 1 :]
     outs, (left, spectra, totals) = rest[: len(far)], rest[len(far) :]
-    count = sum(map(len, early)) + len(late)
     near = [s for s in range(count) if s not in far]
     me = me_ref[0]
     double, length = arrived[0].shape
     part = double // 2
-    for group, one in zip(early, known):
-        for e, s in enumerate(group):
-            spectra[jnp.bitwise_xor(me, s)] = one[e * double : (e + 1) * double, :]
     rows = jnp.concatenate([ref[...] for ref in arrived], axis=0)
     high, low = halves(rows)
     result = dot_split(high, low, fwd_high[...], fwd_low[...])
@@ -194,23 +192,25 @@
         left[e * part : (e + 1) * part, :] = totals[jnp.bitwise_xor(me, s)]
 
 
-def convolve(me, early, late, far, known, arrived, forward, inverse):
-    count = sum(map(len, early)) + len(late)
+def convolve(me, late, far, arrived, spectra, forward, inverse):
+    count = spectra.shape[0]
     double, length = arrived[0].shape
     part = double // 2
     vmem = pl.BlockSpec(memory_space=pltpu.VMEM)
-    return call(
-        functools.partial(conv_body, early, late, far),
+    *pieces, left, _ = call(
+        functools.partial(conv_body, late, far, count),
         [jax.ShapeDtypeStruct((part, length), f32)] * len(far)
-        + [jax.ShapeDtypeStruct(((count - len(far)) * part, 2 * length), f32)],
-        in_specs=[pl.BlockSpec(memory_space=pltpu.SMEM)] + [vmem] * (4 + len(late) + len(early)),
-        out_specs=[vmem] * (len(far) + 1),
-        scratch=[
-            pltpu.VMEM((count, double, 2 * length), f32),
-            pltpu.VMEM((count, part, 2 * length), f32),
+        + [
+            jax.ShapeDtypeStruct(((count - len(far)) * part, 2 * length), f32),
+            jax.ShapeDtypeStruct(spectra.shape, f32),
         ],
+        in_specs=[pl.BlockSpec(memory_space=pltpu.SMEM)] + [vmem] * (5 + len(late)),
+        out_specs=[vmem] * (len(far) + 2),
+        scratch=[pltpu.VMEM((count, part, 2 * length), f32)],
         room=24,
-    )(me, *forward, *inverse, *arrived, *known)
+        aliases={5 + len(late): len(far) + 1},
+    )(me, *forward, *inverse, *arrived, spectra)
+    return pieces, left
 
 
 def restore_body(left, inv_high, inv_low, *outs):
@@ -233,33 +233,34 @@
     )(left, *inverse)
 
 
-def gates_body(count, chunks, me_ref, query_ref, key_ref, value_ref, skip_ref, gate_ref, direct_ref, gate_t, direct_t):
+def gates_body(count, units, me_ref, query_ref, key_ref, value_ref, skip_ref, *refs):
+    outs, (gate_t, direct_t) = refs[:-2], refs[-2:]
     query = query_ref[...]
     gate_t[...] = query.T
     direct_t[...] = (query * (skip_ref[...] * (key_ref[...] * value_ref[...]))).T
-    slim = gate_t.shape[0] // count
-    part = slim // chunks
-    for k in range(chunks):
-        for s in range(count):
-            start = jnp.bitwise_xor(me_ref[0], s) * slim + k * part
-            source = pl.ds(pl.multiple_of(start, 8), part)
-            here = pl.ds((k * count + s) * part, part)
-            gate_ref[here, :] = gate_t[source, :]
-            direct_ref[here, :] = direct_t[source, :]
-
-
-def gates(me, query_rows, key_rows, value_rows, skip_gain, count, chunks):
+    part = gate_t.shape[0] // count
+    for u, unit in enumerate(units):
+        for e, s in enumerate(unit):
+            source = pl.ds(pl.multiple_of(jnp.bitwise_xor(me_ref[0], s) * part, 8), part)
+            here = pl.ds(e * part, part)
+            outs[2 * u][here, :] = gate_t[source, :]
+            outs[2 * u + 1][here, :] = direct_t[source, :]
+
+
+def gates(me, query_rows, key_rows, value_rows, skip_gain, count, units):
     length, channels = query_rows.shape
-    vmem = pl.BlockSpec(memory_space=pltpu.VMEM)
-    return call(
-        functools.partial(gates_body, count, chunks),
-        [jax.ShapeDtypeStruct((channels, length), f32)] * 2,
+    part = channels // count
+    vmem = pl.BlockSpec(memory_space=pltpu.VMEM)
+    flat = call(
+        functools.partial(gates_body, count, units),
+        [jax.ShapeDtypeStruct((len(unit) * part, length), f32) for unit in units for _ in range(2)],
         in_specs=[pl.BlockSpec(memory_space=pltpu.SMEM)] + [vmem] * 4,
-        out_specs=[vmem] * 2,
+        out_specs=[vmem] * (2 * len(units)),
         scratch=[pltpu.VMEM((channels, length), f32)] * 2,
         room=16,
-        work=8 * 10**10,
+        work=80 * 10**9,
     )(me, query_rows, key_rows, value_rows, skip_gain[None, :])
+    return [flat[2 * u : 2 * u + 2] for u in range(len(units))]
 
 
 def mix_body(first, chained, *refs):
@@ -267,24 +268,24 @@
     *pieces, gate, direct = refs[: len(refs) - 2 - chained]
     part = pieces[0].shape[0]
     for e, piece in enumerate(pieces):
-        rows = pl.ds((first + e) * part, part)
-        mixed = gate[rows, :] * piece[...] + direct[rows, :]
-        out[e * part : (e + 1) * part, :] = mixed
-        whole[rows, :] = mixed
-
-
-def mix(pieces, gate, direct, first, whole):
+        here = pl.ds(e * part, part)
+        mixed = gate[here, :] * piece[...] + direct[here, :]
+        out[here, :] = mixed
+        whole[pl.ds((first + e) * part, part), :] = mixed
+
+
+def mix(pieces, gate, direct, first, count, whole):
     part, length = pieces[0].shape
-    count = len(pieces)
+    held = len(pieces)
     vmem = pl.BlockSpec(memory_space=pltpu.VMEM)
     chained = [] if whole is None else [whole]
     return call(
         functools.partial(mix_body, first, len(chained)),
-        [jax.ShapeDtypeStruct((count * part, length), f32), jax.ShapeDtypeStruct(gate.shape, f32)],
-        in_specs=[vmem] * (count + 2 + len(chained)),
+        [jax.ShapeDtypeStruct((held * part, length), f32), jax.ShapeDtypeStruct((count * part, length), f32)],
+        in_specs=[vmem] * (held + 2 + len(chained)),
         out_specs=[vmem] * 2,
         room=8,
-        aliases={count + 2: 1} if chained else None,
+        aliases={held + 2: 1} if chained else None,
     )(*pieces, gate, direct, *chained)
 
 
@@ -333,7 +334,7 @@
             scratch_shapes=[pltpu.VMEM((channels, width), f32)],
         ),
         room=12,
-        work=3 * 10**10,
+        work=20 * 10**9,
     )(me, mine, blocks)
 
 
@@ -429,20 +430,25 @@
     blocks = cut(after(out_weight, sent[0][half]), peers)
     blocks = lax.all_to_all(blocks, "ch", split_axis=0, concat_axis=0, tiled=True)
 
-    gate, direct = gates(me, query_rows, key_rows, value_rows, skip_gain, count, chunks)
-    early, late = [near], far
     part = slim // chunks
     units = [near, far]
     if half // 2 * part % LANES == 0:
         units = [near, far[: half // 2], far[half // 2 :]]
+    gated = gates(me, query_rows, key_rows, value_rows, skip_gain, count, units)
+    early, late = [near, far[: half // 2]], far[half // 2 :]
     total = None
     tables = None
     for k in range(chunks):
-        known = [spectrum([arrived[k][s] for s in group], forward) for group in early]
+        spectra = None
+        for slots in early:
+            pieces = [arrived[k][s] for s in slots]
+            if spectra is not None:
+                spectra, pieces = lax.optimization_barrier((spectra, pieces))
+            spectra = spectrum(me, slots, pieces, forward, count, spectra)
         last = [arrived[k][s] for s in late]
-        last, known, gate, direct = lax.optimization_barrier((last, known, gate, direct))
+        spectra, last, gated = lax.optimization_barrier((spectra, last, gated))
         back = [None] * count
-        *pieces, left = convolve(me, early, late, far, known, last, forward, inverse)
+        pieces, left = convolve(me, late, far, last, spectra, forward, inverse)
         for s, piece in zip(far, pieces):
             back[s] = swap(piece, "seq", count, s)
         for s, piece in zip(near, restore(left, inverse, half)):
@@ -461,20 +467,20 @@
         for u, unit in enumerate(units):
             pieces = [back[s] for s in unit]
             if u:
-                total = project([entry(own[u - 1], u - 1, 0)], tables, total, work=3 * 10**10)
+                total = project([entry(own[u - 1], u - 1, 0)], tables, total, work=20 * 10**9)
                 total, pieces = lax.optimization_barrier((total, pieces))
-            alone, whole = mix(pieces, gate, direct, unit[0], whole)
+            alone, whole = mix(pieces, *gated[u], unit[0], count, whole)
             own.append(alone)
             far_own.append(swap(alone, "ch", peers, bit))
 
     beside = spread(whole, bit)
     across = [spread(after(x, own[last]), bit) for x in far_own[:last]]
-    total = project([entry(own[last], last, 0), entry(across[0][0], 0, bit)], tables, total, work=3 * 10**10)
-    total = project([(beside[o], 0, channels, o * channels) for o in range(1, bit)], tables, total, work=3 * 10**10)
+    total = project([entry(own[last], last, 0), entry(across[0][0], 0, bit)], tables, total, work=20 * 10**9)
+    total = project([(beside[o], 0, channels, o * channels) for o in range(1, bit)], tables, total, work=20 * 10**9)
     if last > 1:
         entries = [entry(across[u][0], u, bit) for u in range(1, last)]
         entries += [entry(across[u][o], u, bit | o) for u in range(last - 1) for o in range(1, bit)]
-        total = project(entries, tables, total, work=3 * 10**10)
+        total = project(entries, tables, total, work=20 * 10**9)
     total, ending = lax.optimization_barrier((total, far_own[last]))
     ending = spread(ending, bit)
     entries = [entry(ending[0], last, bit)]

time: 103 us -> 101 us (0.981)
  waiting for transfers between devices: 26.5 us -> 31.5 us
  starting transfers between devices: 36.7 us -> 34.2 us
  Pallas kernels: 31.1 us -> 28.9 us
  local copies, waits for them, and re-layouts: 7.46 us -> 6.05 us
    ppermute x21, waiting for transfers between devices: 26.5 us -> 31.5 us  [swap(): return lax.ppermute(x, axis, [(j, j ^ offset) for j in range(size)])]
    ppermute x21, starting transfers between devices: 31.7 us -> 29.2 us  [swap(): return lax.ppermute(x, axis, [(j, j ^ offset) for j in range(size)])]
    pallas_call x3, Pallas kernels: 2.92 us -> 0.98 us  [mix(): call(functools.partial(mix_body, first, len(chained)), [jax.ShapeDtypeStr...]
    unnamed x30 -> x42, local copies, waits for them, and re-layouts: 7.46 us -> 6.05 us
    pallas_call x3 -> x4, Pallas kernels: 9.22 us -> 9.9 us  [the longest x1 5.36 us: convolve(): call(functools.partial(conv_body, late, far, count), [jax.ShapeDtypeStruc...]
  transfers between devices with their start and end apart: 22 -> 22, of which waited for: 5 -> 7; matrix products, arithmetic and copies ran while one was open for 0% -> 0% of each run, Pallas kernels for 26% -> 24%
where the time goes in v2:
time: 101 us
  starting transfers between devices  34.2 us (34%)
  waiting for transfers between devices  31.5 us (31%)
  Pallas kernels  28.9 us (29%)
  local copies, waits for them, and re-layouts  6.05 us (6%)
    ppermute x21, waiting for transfers between devices, swap(): return lax.ppermute(x, axis, [(j, j ^ offset) for j in range(size)])  31.5 us
    ppermute x21, starting transfers between devices, swap(): return lax.ppermute(x, axis, [(j, j ^ offset) for j in range(size)])  29.2 us
    pallas_call x7, Pallas kernels, project(): call(functools.partial(project_body, places, started, final), jax.ShapeDt...  7.16 us
    unnamed x42, local copies, waits for them, and re-layouts  6.05 us
    pallas_call x1, Pallas kernels, convolve(): call(functools.partial(conv_body, late, far, count), [jax.ShapeDtypeStruc...  5.36 us
    all_to_all x1, starting transfers between devices, per_device(): lax.all_to_all(blocks, 'ch', split_axis=0, concat_axis=0, tiled=True)  4.99 us
    pallas_call x1, Pallas kernels, weights(): call(functools.partial(weights_body, count, chunks), [jax.ShapeDtypeStruc...  3.83 us
    pallas_call x2, Pallas kernels, spectrum(): call(functools.partial(spectrum_body, slots, len(chained)), jax.ShapeDtyp...  3.82 us
  transfers between devices with their start and end apart: 22, of which 7 were waited for; matrix products, arithmetic and copies ran while one was open for 0% of the time, Pallas kernels for 24%

profile of v2, /device:TPU:0, one launch (start us, length us, event | category | flops | bytes accessed | tf_op | source)
XLA Modules:
  0.0 100.9 jit_solution(4509998647546772277)
XLA Ops:
  0.0 3.0 %shard_map.100 = (f32[128,512]{1,0:T(8,128)S(1)}, f32[128,512]{1,0:T(8,128)S(1)}, f32[128,512]{1,0:T(8,128)S(1)}, f32[128,512]{1,0:T(8,128)}, f32[128,512]{1,0:T...) custom-call(s32[1]{0:T(128)} %bitcast.me_ref, f32[512,512]{1,0:T(8,128)} %key_ref.1, ...), custom_call_target="tpu_custom_call" | custom-call | flops 1 | bytes 1 | tf_op jit(solution)/shard_map/pallas_call | solution.py:96
  3.0 0.7 copy-done.13
  3.7 3.0 %collective-permute-start.1 = (f32[128,512]{1,0:T(8,128)S(1)}, f32[128,512]{1,0:T(8,128)S(1)}, u32[]{:S(2)}, u32[]{:S(2)}) collective-permute-start(f32[128,512]{1,0:T(8,128)S(1)} %get-tuple-element.63), channel_id=1, source_target_pairs={{0,8},{4,12},{8,0},{12,4},{16,24},{20,28},{24,16},{28,20},{1,9},{5... | collective-permute-start | bytes 786440 | tf_op jit(solution)/shard_map/ppermute | solution.py:393
  6.8 1.5 %collective-permute-start = (f32[128,512]{1,0:T(8,128)S(1)}, f32[128,512]{1,0:T(8,128)S(1)}, u32[]{:S(2)}, u32[]{:S(2)}) collective-permute-start(f32[128,512]{1,0:T(8,128)S(1)} %get-tuple-element.62), channel_id=1, source_target_pairs={{0,4},{4,0},{8,12},{12,8},{16,20},{20,16},{24,28},{28,24},{1,5},{5... | collective-permute-start | bytes 786440 | tf_op jit(solution)/shard_map/ppermute | solution.py:393
  8.3 2.5 %collective-permute-start.4 = (f32[128,512]{1,0:T(8,128)}, f32[128,512]{1,0:T(8,128)}, u32[]{:S(2)}, u32[]{:S(2)}) collective-permute-start(f32[128,512]{1,0:T(8,128)} %get-tuple-element.67), channel_id=1, source_target_pairs={{0,20},{4,16},{8,28},{12,24},{16,4},{20,0},{24,12},{28,8},{1,21},{... | collective-permute-start | bytes 786440 | tf_op jit(solution)/shard_map/ppermute | solution.py:393
  10.8 1.9 %collective-permute-start.3 = (f32[128,512]{1,0:T(8,128)}, f32[128,512]{1,0:T(8,128)}, u32[]{:S(2)}, u32[]{:S(2)}) collective-permute-start(f32[128,512]{1,0:T(8,128)} %get-tuple-element.66), channel_id=1, source_target_pairs={{0,16},{4,20},{8,24},{12,28},{16,0},{20,4},{24,8},{28,12},{1,17},{... | collective-permute-start | bytes 786440 | tf_op jit(solution)/shard_map/ppermute | solution.py:393
  12.7 3.0 %shard_map.107 = f32[4,512,512]{2,1,0:T(8,128)S(1)} custom-call(f32[512,2048]{1,0:T(8,128)} %weight_ref), custom_call_target="tpu_custom_call" | custom-call | flops 1 | bytes 1 | tf_op jit(solution)/shard_map/pallas_call | solution.py:299
  15.7 2.0 %copy-done = f32[4,512,512]{2,1,0:T(8,128)} copy-done((f32[4,512,512]{2,1,0:T(8,128)}, f32[4,512,512]{2,1,0:T(8,128)S(1)}, u32[]{:S(2)}) %copy-start) | copy-done | bytes 4194328
  17.7 5.0 %all-to-all-start = ((f32[4,512,512]{2,1,0:T(8,128)}), f32[4,512,512]{2,1,0:T(8,128)}, u32[]{:S(2)}, u32[]{:S(2)}) async-start(f32[4,512,512]{2,1,0:T(8,128)} %copy-done), calls=%async_computation | async-start | bytes 8388608 | tf_op jit(solution)/shard_map/all_to_all | solution.py:431
  22.8 0.7 copy-done.15
  23.4 2.9 %collective-permute-start.6 = (f32[128,512]{1,0:T(8,128)}, f32[128,512]{1,0:T(8,128)S(1)}, u32[]{:S(2)}, u32[]{:S(2)}) collective-permute-start(f32[128,512]{1,0:T(8,128)} %get-tuple-element.72), channel_id=1, source_target_pairs={{0,28},{4,24},{8,20},{12,16},{16,12},{20,8},{24,4},{28,0},{1,29},{... | collective-permute-start | bytes 786440 | tf_op jit(solution)/shard_map/ppermute | solution.py:393
  26.3 0.7 copy-done.17
  27.0 0.6 collective-permute-start.2
  27.6 1.2 %copy-done.19 = f32[512,512]{1,0:T(8,128)S(1)} copy-done((f32[512,512]{1,0:T(8,128)S(1)}, f32[512,512]{1,0:T(8,128)}, u32[]{:S(2)}) %copy-start.19) | copy-done | bytes 1048600
  28.8 0.7 shard_map.103
  29.6 0.7 copy-done.11
  30.2 13.5 %collective-permute-done.2.refs_3_ = f32[128,512]{1,0:T(8,128)S(1)} collective-permute-done((f32[128,512]{1,0:T(8,128)}, f32[128,512]{1,0:T(8,128)S(1)}, u32[]{:S(2)}, u32[]{:S(2)}) %collective-permute-start.2) | collective-permute-done | bytes 262176 | tf_op jit(solution)/shard_map/ppermute | solution.py:393
  43.8 1.8 %shard_map.101.refs_2_ = f32[8,128,1024]{2,1,0:T(8,128)S(1)} custom-call(s32[1]{0:T(128)} %bitcast.me_ref, bf16[512,1024]{1,0:T(8,128)(2,1)S(1)} %copy-done.2, bf16[512,1024]{1,0:T(8,128)(2,1)S(1)} %copy-done.1, f32[128,512]{1,0:T(8,128)S(1)} %copy-done.14, f32[128,512]{1,0:T(8,128)S(1)} %copy-done.18, f32[128,512]{1,0:T(8,128)S(1)} %copy-done.16, ...), custom_call_target="tpu_custom_call" | custom-call | flops 1 | bytes 1 | tf_op jit(solution)/shard_map/pallas_call | solution.py:125
  45.6 0.0 copy-start.3
  45.6 0.0 copy-start.4
  45.6 6.8 %collective-permute-done.3.refs_0_ = f32[128,512]{1,0:T(8,128)} collective-permute-done((f32[128,512]{1,0:T(8,128)}, f32[128,512]{1,0:T(8,128)}, u32[]{:S(2)}, u32[]{:S(2)}) %collective-permute-start.3) | collective-permute-done | bytes 262176 | tf_op jit(solution)/shard_map/ppermute | solution.py:393
  52.4 2.0 %shard_map.102.rest_2_ = f32[8,128,1024]{2,1,0:T(8,128)S(1)} custom-call(s32[1]{0:T(128)} %bitcast.me_ref, bf16[512,1024]{1,0:T(8,128)(2,1)S(1)} %copy-done.2, bf16[512,1024]{1,0:T(8,128)(2,1)S(1)} %copy-done.1, f32[128,512]{1,0:T(8,128)} %collective-permute-done.3.refs_0_, ...), custom_call_target="tpu_custom_call", output_to_operand_aliasing={{}: (5, {})} | custom-call | flops 1 | bytes 1 | tf_op jit(solution)/shard_map/pallas_call | solution.py:125
  54.5 5.4 %shard_map.104 = (f32[64,512]{1,0:T(8,128)}, f32[64,512]{1,0:T(8,128)}, f32[64,512]{1,0:T(8,128)}, f32[64,512]{1,0:T(8,128)S(1)}, f32[256,1024]{1,0:T(8,128)S(1)}, /*index=5*/f32[8,128,1024]{2,1,0:T(8,128)S(1)}) custom-call(s32[1]{0:T(128)} %bitcast.me_ref, bf16[512,1024]{1,0:T(8,128)(2,1)S(1)} %copy-done.2, ...), custom_call_target="tpu_custom_call", output_to_operand_aliasing={{5}: (7, {})} | custom-call | flops 1 | bytes 1 | tf_op jit(solution)/shard_map/pallas_call | solution.py:200
  59.9 1.0 shard_map.105
  60.8 1.6 %collective-permute-start.7 = (f32[64,512]{1,0:T(8,128)S(1)}, f32[64,512]{1,0:T(8,128)S(1)}, u32[]{:S(2)}, u32[]{:S(2)}) collective-permute-start(f32[64,512]{1,0:T(8,128)S(1)} %get-tuple-element.84), channel_id=1, source_target_pairs={{0,4},{4,0},{8,12},{12,8},{16,20},{20,16},{24,28},{28,24},{1,5},{5... | collective-permute-start | bytes 393224 | tf_op jit(solution)/shard_map/ppermute | solution.py:393
  62.4 2.2 %collective-permute-start.8 = (f32[64,512]{1,0:T(8,128)S(1)}, f32[64,512]{1,0:T(8,128)S(1)}, u32[]{:S(2)}, u32[]{:S(2)}) collective-permute-start(f32[64,512]{1,0:T(8,128)S(1)} %get-tuple-element.85), channel_id=1, source_target_pairs={{0,8},{4,12},{8,0},{12,4},{16,24},{20,28},{24,16},{28,20},{1,9},{5... | collective-permute-start | bytes 393224 | tf_op jit(solution)/shard_map/ppermute | solution.py:393
  64.7 0.9 collective-permute-start.9
  65.6 3.0 %collective-permute-start.10 = (f32[64,512]{1,0:T(8,128)}, f32[64,512]{1,0:T(8,128)S(1)}, u32[]{:S(2)}, u32[]{:S(2)}) collective-permute-start(f32[64,512]{1,0:T(8,128)} %get-tuple-element.94), channel_id=1, source_target_pairs={{0,16},{4,20},{8,24},{12,28},{16,0},{20,4},{24,8},{28,12},{1,17},{... | collective-permute-start | bytes 393224 | tf_op jit(solution)/shard_map/ppermute | solution.py:393
  68.7 2.4 %collective-permute-start.12 = (f32[64,512]{1,0:T(8,128)}, f32[64,512]{1,0:T(8,128)S(1)}, u32[]{:S(2)}, u32[]{:S(2)}) collective-permute-start(f32[64,512]{1,0:T(8,128)} %get-tuple-element.103), channel_id=1, source_target_pairs={{0,24},{4,28},{8,16},{12,20},{16,8},{20,12},{24,0},{28,4},{1,25},{... | collective-permute-start | bytes 393224 | tf_op jit(solution)/shard_map/ppermute | solution.py:393
  71.0 2.5 %collective-permute-start.13 = (f32[64,512]{1,0:T(8,128)S(1)}, f32[64,512]{1,0:T(8,128)S(1)}, u32[]{:S(2)}, u32[]{:S(2)}) collective-permute-start(f32[64,512]{1,0:T(8,128)S(1)} %get-tuple-element.104), channel_id=1, source_target_pairs={{0,28},{4,24},{8,20},{12,16},{16,12},{20,8},{24,4},{28,0},{1,29},{... | collective-permute-start | bytes 393224 | tf_op jit(solution)/shard_map/ppermute | solution.py:393
  73.5 0.9 shard_map.106
  74.4 1.5 %collective-permute-start.14 = (f32[256,512]{1,0:T(8,128)}, f32[256,512]{1,0:T(8,128)S(1)}, u32[]{:S(2)}, u32[]{:S(2)}) collective-permute-start(f32[256,512]{1,0:T(8,128)} %get-tuple-element.89.refs_0_), channel_id=1, source_target_pairs={{0,2},{1,3},{2,0},{3,1},{4,6},{5,7},{6,4},{7,5},{8,10},{9,11},{10,... | collective-permute-start | bytes 1572872 | tf_op jit(solution)/shard_map/ppermute | solution.py:393
  75.9 3.8 %shard_map.108 = (bf16[512,2048]{1,0:T(8,128)(2,1)S(1)}, bf16[512,2048]{1,0:T(8,128)(2,1)S(1)}) custom-call(s32[1]{0:T(128)} %bitcast.me_ref, s32[1]{0:T(128)} %bitcast.2.mine_ref, f32[4,512,512]{2,1,0:T(8,128)} %all-to-all-done.weight_ref), custom_call_target="tpu_custom_call" | custom-call | flops 20000000000 | bytes 1 | tf_op jit(solution)/shard_map/pallas_call | solution.py:326
  79.7 1.7 %shard_map.109.refs_0_ = f32[512,512]{1,0:T(8,128)S(1)} custom-call(f32[256,512]{1,0:T(8,128)} %get-tuple-element.89.refs_0_, bf16[512,2048]{1,0:T(8,128)(2,1)S(1)} %get-tuple-element.92.refs_1_.refs_2_.refs_3_, bf16[512,2048]{1,0:T(8,128)(2,1)S(1)} %get-tuple-element.93.refs_2_.refs_3_.refs_4_), custom_call_target="tpu_custom_call" | custom-call | flops 20000000000 | bytes 1 | tf_op jit(solution)/shard_map/pallas_call | solution.py:381
  81.4 2.1 %collective-permute-done.10.refs_0_ = f32[64,512]{1,0:T(8,128)S(1)} collective-permute-done((f32[64,512]{1,0:T(8,128)}, f32[64,512]{1,0:T(8,128)S(1)}, u32[]{:S(2)}, u32[]{:S(2)}) %collective-permute-start.10) | collective-permute-done | bytes 131104 | tf_op jit(solution)/shard_map/ppermute | solution.py:393
  83.5 3.1 %collective-permute-done.11.refs_1_ = f32[64,512]{1,0:T(8,128)S(1)} collective-permute-done((f32[64,512]{1,0:T(8,128)}, f32[64,512]{1,0:T(8,128)S(1)}, u32[]{:S(2)}, u32[]{:S(2)}) %collective-permute-start.11) | collective-permute-done | bytes 131104 | tf_op jit(solution)/shard_map/ppermute | solution.py:393
  86.7 1.6 %collective-permute-start.16 = (f32[128,512]{1,0:T(8,128)S(1)}, f32[128,512]{1,0:T(8,128)S(1)}, u32[]{:S(2)}, u32[]{:S(2)}) collective-permute-start(f32[128,512]{1,0:T(8,128)S(1)} %get-tuple-element.102.refs_1_), channel_id=1, source_target_pairs={{0,2},{1,3},{2,0},{3,1},{4,6},{5,7},{6,4},{7,5},{8,10},{9,11},{10,... | collective-permute-start | bytes 786440 | tf_op jit(solution)/shard_map/ppermute | solution.py:393
  88.3 0.6 shard_map.111.refs_0_
  89.0 0.6 collective-permute-start.18
  89.6 0.5 collective-permute-start.15
  90.1 1.0 shard_map.113.refs_0_
  91.1 4.2 %collective-permute-done.16.refs_1_ = f32[128,512]{1,0:T(8,128)S(1)} collective-permute-done((f32[128,512]{1,0:T(8,128)S(1)}, f32[128,512]{1,0:T(8,128)S(1)}, u32[]{:S(2)}, u32[]{:S(2)}) %collective-permute-start.16) | collective-permute-done | bytes 262176 | tf_op jit(solution)/shard_map/ppermute | solution.py:393
  95.3 1.0 shard_map.114.refs_0_
  96.3 1.0 shard_map.115.refs_0_
  97.3 0.8 collective-permute-done.18.refs_1_
  98.1 0.6 shard_map.116.refs_0_
  98.7 0.9 collective-permute-done.20.refs_1_
  99.6 1.3 %shard_map.117 = f32[512,512]{1,0:T(8,128)} custom-call(f32[512,512]{1,0:T(8,128)S(1)} %shard_map.116.refs_0_, f32[128,512]{1,0:T(8,128)S(1)} %collective-permute-done.20.refs_1_, bf16[512,2048]{1,0:T(8,128)(2,1)S(1)} %get-tuple-element.92.refs_1_.refs_2_.refs_3_, bf16[512,2048]{1,0:T(8,128)(2,1)S(1)} %get-tuple-element.93.refs_2_.refs_3_.refs_4_), custom_call_target="tpu_custom_call" | custom-call | flops 1 | bytes 1 | tf_op jit(solution)/shard_map/pallas_call | solution.py:381
  (56 shorter events, 0.2 us)
Async XLA Ops:
  3.0 0.7 copy-start.13
  3.7 19.0 %collective-permute-start.1 = (f32[128,512]{1,0:T(8,128)S(1)}, f32[128,512]{1,0:T(8,128)S(1)}, u32[]{:S(2)}, u32[]{:S(2)}) collective-permute-start(f32[128,512]{1,0:T(8,128)S(1)} %get-tuple-element.63), channel_id=1, source_target_pairs={{0,8},{4,12},{8,0},{12,4},{16,24},{20,28},{24,16},{28,20},{1,9},{5... | collective-permute-start | bytes 786440 | tf_op jit(solution)/shard_map/ppermute | solution.py:393
  6.8 19.5 %collective-permute-start = (f32[128,512]{1,0:T(8,128)S(1)}, f32[128,512]{1,0:T(8,128)S(1)}, u32[]{:S(2)}, u32[]{:S(2)}) collective-permute-start(f32[128,512]{1,0:T(8,128)S(1)} %get-tuple-element.62), channel_id=1, source_target_pairs={{0,4},{4,0},{8,12},{12,8},{16,20},{20,16},{24,28},{28,24},{1,5},{5... | collective-permute-start | bytes 786440 | tf_op jit(solution)/shard_map/ppermute | solution.py:393
  8.3 37.3 %collective-permute-start.4 = (f32[128,512]{1,0:T(8,128)}, f32[128,512]{1,0:T(8,128)}, u32[]{:S(2)}, u32[]{:S(2)}) collective-permute-start(f32[128,512]{1,0:T(8,128)} %get-tuple-element.67), channel_id=1, source_target_pairs={{0,20},{4,16},{8,28},{12,24},{16,4},{20,0},{24,12},{28,8},{1,21},{... | collective-permute-start | bytes 786440 | tf_op jit(solution)/shard_map/ppermute | solution.py:393
  10.8 43.7 %collective-permute-start.5 = (f32[128,512]{1,0:T(8,128)}, f32[128,512]{1,0:T(8,128)}, u32[]{:S(2)}, u32[]{:S(2)}) collective-permute-start(f32[128,512]{1,0:T(8,128)} %get-tuple-element.71), channel_id=1, source_target_pairs={{0,24},{4,28},{8,16},{12,20},{16,8},{20,12},{24,0},{28,4},{1,25},{... | collective-permute-start | bytes 786440 | tf_op jit(solution)/shard_map/ppermute | solution.py:393
  10.8 41.6 %collective-permute-start.3 = (f32[128,512]{1,0:T(8,128)}, f32[128,512]{1,0:T(8,128)}, u32[]{:S(2)}, u32[]{:S(2)}) collective-permute-start(f32[128,512]{1,0:T(8,128)} %get-tuple-element.66), channel_id=1, source_target_pairs={{0,16},{4,20},{8,24},{12,28},{16,0},{20,4},{24,8},{28,12},{1,17},{... | collective-permute-start | bytes 786440 | tf_op jit(solution)/shard_map/ppermute | solution.py:393
  15.7 2.0 %copy-start = (f32[4,512,512]{2,1,0:T(8,128)}, f32[4,512,512]{2,1,0:T(8,128)S(1)}, u32[]{:S(2)}) copy-start(f32[4,512,512]{2,1,0:T(8,128)S(1)} %shard_map.107) | copy-start | bytes 12582916
  17.7 9.8 %copy-start.5 = (f32[512,512]{1,0:T(8,128)S(1)}, f32[512,512]{1,0:T(8,128)}, u32[]{:S(2)}) copy-start(f32[512,512]{1,0:T(8,128)} %key_ref.1) | copy-start | bytes 3145732
  17.7 9.8 %copy-start.6 = (f32[512,512]{1,0:T(8,128)S(1)}, f32[512,512]{1,0:T(8,128)}, u32[]{:S(2)}) copy-start(f32[512,512]{1,0:T(8,128)} %value_ref.1) | copy-start | bytes 3145732
  17.7 9.8 %copy-start.20 = (f32[512]{0:T(512)S(1)}, f32[512]{0:T(512)}, u32[]{:S(2)}) copy-start(f32[512]{0:T(512)} %param.14) | copy-start | bytes 6148
  17.7 58.2 %all-to-all-start = ((f32[4,512,512]{2,1,0:T(8,128)}), f32[4,512,512]{2,1,0:T(8,128)}, u32[]{:S(2)}, u32[]{:S(2)}) async-start(f32[4,512,512]{2,1,0:T(8,128)} %copy-done), calls=%async_computation | async-start | bytes 8388608 | tf_op jit(solution)/shard_map/all_to_all | solution.py:431
  22.7 0.7 copy-start.15
  23.4 31.0 %collective-permute-start.6 = (f32[128,512]{1,0:T(8,128)}, f32[128,512]{1,0:T(8,128)S(1)}, u32[]{:S(2)}, u32[]{:S(2)}) collective-permute-start(f32[128,512]{1,0:T(8,128)} %get-tuple-element.72), channel_id=1, source_target_pairs={{0,28},{4,24},{8,20},{12,16},{16,12},{20,8},{24,4},{28,0},{1,29},{... | collective-permute-start | bytes 786440 | tf_op jit(solution)/shard_map/ppermute | solution.py:393
  26.3 0.7 copy-start.17
  27.0 16.7 %collective-permute-start.2 = (f32[128,512]{1,0:T(8,128)}, f32[128,512]{1,0:T(8,128)S(1)}, u32[]{:S(2)}, u32[]{:S(2)}) collective-permute-start(f32[128,512]{1,0:T(8,128)} %get-tuple-element.65), channel_id=1, source_target_pairs={{0,12},{4,8},{8,4},{12,0},{16,28},{20,24},{24,20},{28,16},{1,13},{... | collective-permute-start | bytes 786440 | tf_op jit(solution)/shard_map/ppermute | solution.py:393
  27.6 1.2 %copy-start.19 = (f32[512,512]{1,0:T(8,128)S(1)}, f32[512,512]{1,0:T(8,128)}, u32[]{:S(2)}) copy-start(f32[512,512]{1,0:T(8,128)} %query_ref.1) | copy-start | bytes 3145732
  28.8 14.9 %copy-start.1 = (bf16[512,1024]{1,0:T(8,128)(2,1)S(1)}, bf16[512,1024]{1,0:T(8,128)(2,1)}, u32[]{:S(2)}) copy-start(bf16[512,1024]{1,0:T(8,128)(2,1)} %constant.18.clone.fwd_low) | copy-start | bytes 3145732
  28.8 14.9 %copy-start.2 = (bf16[512,1024]{1,0:T(8,128)(2,1)S(1)}, bf16[512,1024]{1,0:T(8,128)(2,1)}, u32[]{:S(2)}) copy-start(bf16[512,1024]{1,0:T(8,128)(2,1)} %constant.17.clone.fwd_high) | copy-start | bytes 3145732
  28.8 14.9 %copy-start.14 = (f32[128,512]{1,0:T(8,128)S(1)}, f32[128,512]{1,0:T(8,128)}, u32[]{:S(2)}) copy-start(f32[128,512]{1,0:T(8,128)} %copy-done.13) | copy-start | bytes 786436
  28.8 14.9 %copy-start.16 = (f32[128,512]{1,0:T(8,128)S(1)}, f32[128,512]{1,0:T(8,128)}, u32[]{:S(2)}) copy-start(f32[128,512]{1,0:T(8,128)} %copy-done.15) | copy-start | bytes 786436
  28.8 14.9 %copy-start.18 = (f32[128,512]{1,0:T(8,128)S(1)}, f32[128,512]{1,0:T(8,128)}, u32[]{:S(2)}) copy-start(f32[128,512]{1,0:T(8,128)} %copy-done.17) | copy-start | bytes 786436
  29.5 0.7 copy-start.11
  30.2 24.2 %copy-start.7 = (f32[128,512]{1,0:T(8,128)}, f32[128,512]{1,0:T(8,128)S(1)}, u32[]{:S(2)}) copy-start(f32[128,512]{1,0:T(8,128)S(1)} %get-tuple-element.109.refs_3_) | copy-start | bytes 786436
  30.2 24.2 %copy-start.9 = (f32[128,512]{1,0:T(8,128)}, f32[128,512]{1,0:T(8,128)S(1)}, u32[]{:S(2)}) copy-start(f32[128,512]{1,0:T(8,128)S(1)} %get-tuple-element.99.refs_2_) | copy-start | bytes 786436
  45.6 8.9 %copy-start.3 = (bf16[1024,512]{1,0:T(8,128)(2,1)S(1)}, bf16[1024,512]{1,0:T(8,128)(2,1)}, u32[]{:S(2)}) copy-start(bf16[1024,512]{1,0:T(8,128)(2,1)} %constant.20.clone.inv_low) | copy-start | bytes 3145732
  45.6 8.9 %copy-start.4 = (bf16[1024,512]{1,0:T(8,128)(2,1)S(1)}, bf16[1024,512]{1,0:T(8,128)(2,1)}, u32[]{:S(2)}) copy-start(bf16[1024,512]{1,0:T(8,128)(2,1)} %constant.19.clone.inv_high) | copy-start | bytes 3145732
  60.8 7.8 %collective-permute-start.7 = (f32[64,512]{1,0:T(8,128)S(1)}, f32[64,512]{1,0:T(8,128)S(1)}, u32[]{:S(2)}, u32[]{:S(2)}) collective-permute-start(f32[64,512]{1,0:T(8,128)S(1)} %get-tuple-element.84), channel_id=1, source_target_pairs={{0,4},{4,0},{8,12},{12,8},{16,20},{20,16},{24,28},{28,24},{1,5},{5... | collective-permute-start | bytes 393224 | tf_op jit(solution)/shard_map/ppermute | solution.py:393
  62.4 8.6 %collective-permute-start.8 = (f32[64,512]{1,0:T(8,128)S(1)}, f32[64,512]{1,0:T(8,128)S(1)}, u32[]{:S(2)}, u32[]{:S(2)}) collective-permute-start(f32[64,512]{1,0:T(8,128)S(1)} %get-tuple-element.85), channel_id=1, source_target_pairs={{0,8},{4,12},{8,0},{12,4},{16,24},{20,28},{24,16},{28,20},{1,9},{5... | collective-permute-start | bytes 393224 | tf_op jit(solution)/shard_map/ppermute | solution.py:393
  64.7 8.8 %collective-permute-start.9 = (f32[64,512]{1,0:T(8,128)S(1)}, f32[64,512]{1,0:T(8,128)S(1)}, u32[]{:S(2)}, u32[]{:S(2)}) collective-permute-start(f32[64,512]{1,0:T(8,128)S(1)} %get-tuple-element.86), channel_id=1, source_target_pairs={{0,12},{4,8},{8,4},{12,0},{16,28},{20,24},{24,20},{28,16},{1,13},{... | collective-permute-start | bytes 393224 | tf_op jit(solution)/shard_map/ppermute | solution.py:393
  65.6 17.9 %collective-permute-start.10 = (f32[64,512]{1,0:T(8,128)}, f32[64,512]{1,0:T(8,128)S(1)}, u32[]{:S(2)}, u32[]{:S(2)}) collective-permute-start(f32[64,512]{1,0:T(8,128)} %get-tuple-element.94), channel_id=1, source_target_pairs={{0,16},{4,20},{8,24},{12,28},{16,0},{20,4},{24,8},{28,12},{1,17},{... | collective-permute-start | bytes 393224 | tf_op jit(solution)/shard_map/ppermute | solution.py:393
  68.6 18.0 %collective-permute-start.11 = (f32[64,512]{1,0:T(8,128)}, f32[64,512]{1,0:T(8,128)S(1)}, u32[]{:S(2)}, u32[]{:S(2)}) collective-permute-start(f32[64,512]{1,0:T(8,128)} %get-tuple-element.95), channel_id=1, source_target_pairs={{0,20},{4,16},{8,28},{12,24},{16,4},{20,0},{24,12},{28,8},{1,21},{... | collective-permute-start | bytes 393224 | tf_op jit(solution)/shard_map/ppermute | solution.py:393
  68.7 20.2 %collective-permute-start.12 = (f32[64,512]{1,0:T(8,128)}, f32[64,512]{1,0:T(8,128)S(1)}, u32[]{:S(2)}, u32[]{:S(2)}) collective-permute-start(f32[64,512]{1,0:T(8,128)} %get-tuple-element.103), channel_id=1, source_target_pairs={{0,24},{4,28},{8,16},{12,20},{16,8},{20,12},{24,0},{28,4},{1,25},{... | collective-permute-start | bytes 393224 | tf_op jit(solution)/shard_map/ppermute | solution.py:393
  71.0 17.9 %collective-permute-start.13 = (f32[64,512]{1,0:T(8,128)S(1)}, f32[64,512]{1,0:T(8,128)S(1)}, u32[]{:S(2)}, u32[]{:S(2)}) collective-permute-start(f32[64,512]{1,0:T(8,128)S(1)} %get-tuple-element.104), channel_id=1, source_target_pairs={{0,28},{4,24},{8,20},{12,16},{16,12},{20,8},{24,4},{28,0},{1,29},{... | collective-permute-start | bytes 393224 | tf_op jit(solution)/shard_map/ppermute | solution.py:393
  74.4 15.2 %collective-permute-start.14 = (f32[256,512]{1,0:T(8,128)}, f32[256,512]{1,0:T(8,128)S(1)}, u32[]{:S(2)}, u32[]{:S(2)}) collective-permute-start(f32[256,512]{1,0:T(8,128)} %get-tuple-element.89.refs_0_), channel_id=1, source_target_pairs={{0,2},{1,3},{2,0},{3,1},{4,6},{5,7},{6,4},{7,5},{8,10},{9,11},{10,... | collective-permute-start | bytes 1572872 | tf_op jit(solution)/shard_map/ppermute | solution.py:393
  79.7 6.9 %copy-start.10 = (f32[128,512]{1,0:T(8,128)S(1)}, f32[128,512]{1,0:T(8,128)}, u32[]{:S(2)}) copy-start(f32[128,512]{1,0:T(8,128)} %copy-done.9) | copy-start | bytes 786436
  79.7 6.9 %copy-start.12 = (f32[128,512]{1,0:T(8,128)S(1)}, f32[128,512]{1,0:T(8,128)}, u32[]{:S(2)}) copy-start(f32[128,512]{1,0:T(8,128)} %copy-done.11) | copy-start | bytes 786436
  86.7 2.2 %copy-start.8 = (f32[128,512]{1,0:T(8,128)S(1)}, f32[128,512]{1,0:T(8,128)}, u32[]{:S(2)}) copy-start(f32[128,512]{1,0:T(8,128)} %copy-done.7) | copy-start | bytes 786436
  86.7 8.6 %collective-permute-start.16 = (f32[128,512]{1,0:T(8,128)S(1)}, f32[128,512]{1,0:T(8,128)S(1)}, u32[]{:S(2)}, u32[]{:S(2)}) collective-permute-start(f32[128,512]{1,0:T(8,128)S(1)} %get-tuple-element.102.refs_1_), channel_id=1, source_target_pairs={{0,2},{1,3},{2,0},{3,1},{4,6},{5,7},{6,4},{7,5},{8,10},{9,11},{10,... | collective-permute-start | bytes 786440 | tf_op jit(solution)/shard_map/ppermute | solution.py:393
  89.0 9.1 %collective-permute-start.18 = (f32[128,512]{1,0:T(8,128)S(1)}, f32[128,512]{1,0:T(8,128)S(1)}, u32[]{:S(2)}, u32[]{:S(2)}) collective-permute-start(f32[128,512]{1,0:T(8,128)S(1)} %get-tuple-element.111.refs_1_), channel_id=1, source_target_pairs={{0,2},{1,3},{2,0},{3,1},{4,6},{5,7},{6,4},{7,5},{8,10},{9,11},{10,... | collective-permute-start | bytes 786440 | tf_op jit(solution)/shard_map/ppermute | solution.py:393
  89.6 6.8 %collective-permute-start.17 = (f32[256,512]{1,0:T(8,128)S(1)}, f32[256,512]{1,0:T(8,128)S(1)}, u32[]{:S(2)}, u32[]{:S(2)}) collective-permute-start(f32[256,512]{1,0:T(8,128)S(1)} %collective-permute-done.14.refs_2_), channel_id=1, source_target_pairs={{0,1},{1,0},{2,3},{3,2},{4,5},{5,4},{6,7},{7,6},{8,9},{9,8},{10,11... | collective-permute-start | bytes 1572872 | tf_op jit(solution)/shard_map/ppermute | solution.py:393
  89.6 5.7 %collective-permute-start.15 = (f32[512,512]{1,0:T(8,128)S(1)}, f32[512,512]{1,0:T(8,128)S(1)}, u32[]{:S(2)}, u32[]{:S(2)}) collective-permute-start(f32[512,512]{1,0:T(8,128)S(1)} %get-tuple-element.113), channel_id=1, source_target_pairs={{0,1},{1,0},{2,3},{3,2},{4,5},{5,4},{6,7},{7,6},{8,9},{9,8},{10,11... | collective-permute-start | bytes 3145736 | tf_op jit(solution)/shard_map/ppermute | solution.py:393
  95.3 2.8 %collective-permute-start.19 = (f32[128,512]{1,0:T(8,128)S(1)}, f32[128,512]{1,0:T(8,128)S(1)}, u32[]{:S(2)}, u32[]{:S(2)}) collective-permute-start(f32[128,512]{1,0:T(8,128)S(1)} %collective-permute-done.16.refs_1_), channel_id=1, source_target_pairs={{0,1},{1,0},{2,3},{3,2},{4,5},{5,4},{6,7},{7,6},{8,9},{9,8},{10,11... | collective-permute-start | bytes 786440 | tf_op jit(solution)/shard_map/ppermute | solution.py:393
  98.1 1.5 %collective-permute-start.20 = (f32[128,512]{1,0:T(8,128)S(1)}, f32[128,512]{1,0:T(8,128)S(1)}, u32[]{:S(2)}, u32[]{:S(2)}) collective-permute-start(f32[128,512]{1,0:T(8,128)S(1)} %collective-permute-done.18.refs_1_), channel_id=1, source_target_pairs={{0,1},{1,0},{2,3},{3,2},{4,5},{5,4},{6,7},{7,6},{8,9},{9,8},{10,11... | collective-permute-start | bytes 786440 | tf_op jit(solution)/shard_map/ppermute | solution.py:393
